TPU v7x, 512 devices: a whole 4x4x16 slice. The times are simulated.
512 devices in a mesh: fourier: 16 (over x_hi, y, core), meridian: 32 (over z, x_lo).
Axes of the slice: x: 4 (x_hi: 2, x_lo: 2; x = x_hi * 2 + x_lo), y: 4, z: 16, core: 2. Of those that a mesh axis runs over, the one named last changes fastest.
Arguments:
- forward_now: float32 [3, 4224, 2048], P(None, 'meridian', 'fourier'), may hold values from -3 to 3
- forward_last: float32 [3, 4224, 2048], P(None, 'meridian', 'fourier'), may hold values from -3 to 3
- adjoint_now: float32 [3, 4224, 2048], P(None, 'meridian', 'fourier'), may hold values from -3 to 3
- adjoint_last: float32 [3, 4224, 2048], P(None, 'meridian', 'fourier'), may hold values from -3 to 3
- moduli: float32 [21, 17, 32, 400], P(None, None, 'meridian', 'fourier'), may hold values from -1.8 to 1.8
- inv_radius: float32 [12800], P('meridian'), may hold values from 0.0009765625 to 0.0078125
- inv_mass: float32 [8448], P('meridian'), may hold values from 0.005 to 0.05
Outputs:
- forward_next: float32 [3, 4224, 2048], P(None, 'meridian', 'fourier')
- adjoint_next: float32 [3, 4224, 2048], P(None, 'meridian', 'fourier')
- kernel: float32 [21, 17, 32, 400], P(None, None, 'meridian', 'fourier')
All inputs are finite; a program needn't handle non-finite values.
Results may differ from a plain program's by a relative error of at most 0.0001.
Values sent between devices are 32-bit elements; how exact they have to be, the bound alone decides.
No kernel may reach another device: no remote copies, remote signals or barrier semaphores. Data moves between devices by JAX's collectives and lax.ppermute only.
A program may use at most 64 MiB of HBM per device.

v0:
```python
import math

import jax
import jax.numpy as jnp
import ml_dtypes
import numpy as np
from jax import lax
from jax.experimental import pallas as pl
from jax.experimental.pallas import tpu as pltpu
from jax.sharding import PartitionSpec as P

FOURIER = "fourier"
MERIDIAN = "meridian"
PEERS = 16
OWN = 32
REACH = 8
LANES = 128
TOTAL = 1024
ROWS = 160
NEXT = 136
CHUNK = 40
PART = 80
NODES = 25

f32 = jnp.float32
bf16 = jnp.bfloat16


def wave_rows(f, order):
    if f == 0:
        low = 2.0 * np.pi * np.arange(96) / 96
        high = 2.0 * np.pi * np.arange(32) / 32
        cos_row, sin_row = np.zeros(LANES), np.zeros(LANES)
        if order < TOTAL // 4:
            cos_row[:96], sin_row[:96] = np.cos(order * low), np.sin(order * low)
        else:
            back = TOTAL // 2 - order
            cos_row[96:], sin_row[96:] = np.cos(back * high), -np.sin(back * high)
        return cos_row, sin_row
    angle = 2.0 * np.pi * ((np.arange(64) * (order - OWN * f)) % 64) / 64
    cos_row = 0.5 * np.concatenate([np.cos(angle), np.sin(angle)])
    sin_row = 0.5 * np.concatenate([np.sin(angle), -np.cos(angle)])
    return cos_row, sin_row


def pair_rows(f, order):
    cos_row, sin_row = wave_rows(f, order)
    return [(cos_row, -order * sin_row), (sin_row, order * cos_row)]


def top_row(f):
    row = np.zeros(LANES)
    if f == 0:
        row[96:] = 1.0
    else:
        angle = 2.0 * np.pi * ((np.arange(64) * (TOTAL // 2 - OWN * f)) % 64) / 64
        row[:] = np.concatenate([np.cos(angle), np.sin(angle)])
    return row


def forward_tables():
    tables = np.zeros((PEERS, 2 * LANES, 4 * LANES))

    def put(f, lane, rows):
        for parity in range(2):
            at = lane + parity
            tables[f, at, parity * LANES : (parity + 1) * LANES] = rows[0]
            tables[f, at, (2 + parity) * LANES : (3 + parity) * LANES] = rows[1]

    nothing = np.zeros(LANES)
    for f in range(PEERS):
        for m in range(OWN):
            if f == 0 and m == 0:
                put(f, 0, (wave_rows(0, 0)[0], nothing))
                put(f, 2, (top_row(0), nothing))
                continue
            for part, rows in enumerate(pair_rows(f, OWN * f + m)):
                put(f, 4 * m + 2 * part, rows)
        for m in range(REACH):
            left = (OWN * f - REACH + m) % (TOTAL // 2)
            for part, rows in enumerate(pair_rows(f, left)):
                put(f, LANES + 4 * m + 2 * part, rows)
            if f < PEERS - 1:
                for part, rows in enumerate(pair_rows(f, OWN * f + OWN + m)):
                    put(f, LANES + 32 + 4 * m + 2 * part, rows)
        if f == PEERS - 1:
            put(f, LANES + 32 + 2, (top_row(f), nothing))
            for m in range(1, REACH):
                order = TOTAL // 2 - REACH + m
                angle = 2.0 * np.pi * ((np.arange(64) * (TOTAL - order - OWN * f)) % 64) / 64
                cos_row = 0.5 * np.concatenate([np.cos(angle), np.sin(angle)])
                sin_row = 0.5 * np.concatenate([-np.sin(angle), np.cos(angle)])
                put(f, LANES + 64 + 4 * m, (cos_row, -order * sin_row))
                put(f, LANES + 64 + 4 * m + 2, (sin_row, order * cos_row))
    return tables


def inverse_tables():
    tables = np.zeros((PEERS, 4 * LANES, LANES))

    def put(f, lane, straight, turned):
        for parity in range(2):
            base = 2 * parity * LANES
            tables[f, base : base + LANES, lane + parity] = straight
            tables[f, base + LANES : base + 2 * LANES, lane + parity] = turned

    nothing = np.zeros(LANES)
    for f in range(PEERS):
        for m in range(OWN):
            order = OWN * f + m
            cos_row, sin_row = wave_rows(f, order)
            if f == 0:
                cos_row, sin_row = cos_row / 96, sin_row / 96
            else:
                cos_row, sin_row = cos_row / 32, sin_row / 32
            if order == 0:
                put(f, 0, cos_row, nothing)
                put(f, 2, top_row(0) / 32, nothing)
                continue
            put(f, 4 * m, cos_row, -order * sin_row)
            put(f, 4 * m + 2, sin_row, order * cos_row)
    return tables


def basis_lanes(low):
    if low:
        angles = np.concatenate(
            [2.0 * np.pi * np.arange(96) / 96, 2.0 * np.pi * np.arange(32) / 32]
        )
        share = np.concatenate([np.full(96, TOTAL / 96), np.full(32, TOTAL / 32)])
    else:
        angles = np.tile(2.0 * np.pi * np.arange(64) / 64, 2)
        share = np.full(LANES, TOTAL / 32)
    rows = [np.ones(LANES)]
    for order in range(1, REACH + 1):
        rows += [np.cos(order * angles), np.sin(order * angles)]
    return np.stack(rows), share


def moduli_tables():
    sampling = np.zeros((2, LANES, 7 * LANES))
    projection = np.zeros((2, 7 * LANES, LANES))
    for kind in range(2):
        rows, share = basis_lanes(kind == 0)
        for r in range(7):
            sampling[kind, 17 * r : 17 * r + 17, r * LANES : (r + 1) * LANES] = rows
            projection[kind, r * LANES : (r + 1) * LANES, 17 * r : 17 * r + 17] = (
                0.0001 * (rows * share).T
            )
    return sampling, projection


def in_two(table):
    table = np.asarray(table, np.float64)
    high = table.astype(ml_dtypes.bfloat16)
    low = (table - high.astype(np.float64)).astype(ml_dtypes.bfloat16)
    return high, low


def gll():
    x = np.array([-1.0, -math.sqrt(3.0 / 7.0), 0.0, math.sqrt(3.0 / 7.0), 1.0])
    weights = np.array([0.1, 49.0 / 90.0, 32.0 / 45.0, 49.0 / 90.0, 0.1])
    factor = [np.prod([x[i] - x[k] for k in range(5) if k != i]) for i in range(5)]
    derive = np.zeros((5, 5))
    for i in range(5):
        for k in range(5):
            if i != k:
                derive[i, k] = factor[i] / (factor[k] * (x[i] - x[k]))
            else:
                derive[i, k] = sum(1.0 / (x[i] - x[j]) for j in range(5) if j != i)
    return derive, np.outer(weights, weights).reshape(25)


DERIVE, WEIGHTS = gll()


def apply_line(matrix, x):
    m = matrix
    s0, s1 = x[0] + x[4], x[1] + x[3]
    d0, d1 = x[0] - x[4], x[1] - x[3]
    y = [None] * 5
    for i in range(2):
        even = (
            float(0.5 * (m[i, 0] + m[i, 4])) * s0
            + float(0.5 * (m[i, 1] + m[i, 3])) * s1
            + float(m[i, 2]) * x[2]
        )
        odd = float(0.5 * (m[i, 0] - m[i, 4])) * d0 + float(0.5 * (m[i, 1] - m[i, 3])) * d1
        y[i] = odd + even
        y[4 - i] = odd - even
    y[2] = float(m[2, 0]) * d0 + float(m[2, 1]) * d1
    return y


def halves(x):
    high = x.astype(bf16)
    return high, (x - high.astype(f32)).astype(bf16)


def product(x, high, low):
    x_high, x_low = halves(x)
    return (
        jnp.dot(x_high, high, preferred_element_type=f32)
        + jnp.dot(x_low, high, preferred_element_type=f32)
        + jnp.dot(x_high, low, preferred_element_type=f32)
    )


def voigt(v, w):
    v, w = min(v, w), max(v, w)
    return v * 6 - v * (v - 1) // 2 + w - v


def point_rows(ea, i, j):
    if 4 * ea + i == 8:
        return NEXT + j // 2, j % 2
    at = (4 * ea + i) * 33 + j
    return at // 2, at % 2


def spread_moduli_kernel(moduli_ref, out_ref):
    for t in range(3):
        block = moduli_ref[119 * t : 119 * t + 119, :]
        block = jnp.concatenate([block, jnp.zeros((LANES - 119, NODES), f32)], axis=0)
        turned = jnp.transpose(block)
        for e in range(PEERS):
            out_ref[e, t * NODES : t * NODES + NODES, :] = turned
    for e in range(PEERS):
        out_ref[e, 75:PART, :] = jnp.zeros((PART - 75, LANES), f32)


def pack_kernel(forward_ref, adjoint_ref, next_ref, x_ref, top_ref, low_ref):
    x_ref[0:3, 0:132, :] = forward_ref[...]
    x_ref[3:6, 0:132, :] = adjoint_ref[...]
    x_ref[:, 132:NEXT, :] = jnp.zeros((6, NEXT - 132, LANES), f32)
    x_ref[:, NEXT:ROWS, :] = next_ref[...]
    group = lax.broadcasted_iota(jnp.int32, (CHUNK, LANES), 1) // 32
    for c in range(6):
        low = x_ref[c, 0:CHUNK, :]
        top = pltpu.roll(low, 32, 1)
        for g in range(1, 4):
            rows = x_ref[c, CHUNK * g : CHUNK * g + CHUNK, :]
            low = jnp.where(group == g, pltpu.roll(rows, 32 * g, 1), low)
            top = jnp.where(
                group == g, rows if g == 3 else pltpu.roll(rows, 32 * g + 32, 1), top
            )
        low_ref[c] = low
        top_ref[c] = top


def strain_kernel(
    f_ref,
    x_ref,
    left_ref,
    right_ref,
    top_ref,
    wave_high,
    wave_low,
    project_high,
    project_low,
    radius_ref,
    weight_ref,
    strain_ref,
    terms_ref,
    halo_ref,
    sample_ref,
    central_ref,
    high_ref,
    low_ref,
    sum_ref,
):
    group = lax.broadcasted_iota(jnp.int32, (CHUNK, LANES), 1) // 32
    for c in range(6):
        left, right, top = left_ref[c], right_ref[c], top_ref[c]
        for g in range(4):
            a = left if g == 0 else pltpu.roll(left, (-32 * g) % LANES, 1)
            b = right if g == 1 else pltpu.roll(right, (32 - 32 * g) % LANES, 1)
            d = top if g == 2 else pltpu.roll(top, (64 - 32 * g) % LANES, 1)
            rows = jnp.where(group == 0, a, jnp.where(group == 1, b, d))
            halo_ref[c, CHUNK * g : CHUNK * g + CHUNK, :] = jnp.where(group == 3, 0.0, rows)
    for c in range(6):
        own = product(x_ref[c], wave_high[0, :LANES, :], wave_low[0, :LANES, :])
        beside = product(halo_ref[c], wave_high[0, LANES:, :], wave_low[0, LANES:, :])
        both = own + beside
        for k in range(4):
            sample_ref[c // 3, c % 3, k] = both[:, k * LANES : (k + 1) * LANES]
            if c < 3:
                sample_ref[2, c, k] = own[:, k * LANES : (k + 1) * LANES]

    @pl.loop(0, 3)
    def _(which):
        def strain_of(v):
            return strain_ref.at[which, v]

        for ea in range(2):

            def node(c, turned, i, j):
                row, parity = point_rows(ea, i, j)
                return sample_ref[which, c, 2 * turned + parity, pl.ds(row, 8, stride=2), :]

            def place(i, j):
                return pl.ds((i * 5 + j) * 16 + ea * 8, 8)

            def store(v, i, j, value, add):
                at = (which, v, place(i, j), slice(None))
                if add:
                    value = value + central_ref[at]
                central_ref[at] = value

            for c, v_a, v_b, v_p, add_a, add_b in (
                (0, 0, 5, 4, False, False),
                (1, 5, 1, 3, True, False),
                (2, 4, 3, 2, True, True),
            ):
                for i in range(5):
                    for j in range(5):
                        store(
                            v_p, i, j, radius_ref[place(i, j), :] * node(c, 1, i, j), False
                        )
                for j in range(5):
                    line = apply_line(DERIVE, [node(c, 0, i, j) for i in range(5)])
                    for i in range(5):
                        store(v_a, i, j, line[i], add_a)
                for i in range(5):
                    line = apply_line(DERIVE, [node(c, 0, i, j) for j in range(5)])
                    for j in range(5):
                        store(v_b, i, j, line[j], add_b)

    strain_ref[...] = central_ref[0:2]

    @pl.loop(0, NODES)
    def _(n):
        rows = pl.ds(pl.multiple_of(n * 16, 16), 16)
        a = [central_ref[1, v, rows, :] for v in range(6)]
        f = [central_ref[2, v, rows, :] * weight_ref[n] for v in range(6)]
        for v in range(6):
            for w in range(v, 6):
                term = f[v] * a[w]
                if v != w:
                    term = term + f[w] * a[v]
                r = voigt(v, w)
                high, low = halves(term)
                high_ref[rows, r * LANES : (r + 1) * LANES] = high
                low_ref[rows, r * LANES : (r + 1) * LANES] = low

    for t in range(3):
        cut = slice(t * 7 * LANES, (t + 1) * 7 * LANES)
        high, low = high_ref[:, cut], low_ref[:, cut]
        sum_ref[...] = (
            jnp.dot(high, project_high[0], preferred_element_type=f32)
            + jnp.dot(low, project_high[0], preferred_element_type=f32)
            + jnp.dot(high, project_low[0], preferred_element_type=f32)
        )
        for n in range(NODES):
            for ea in range(2):
                terms_ref[pl.ds(ea * 8 * PART + t * NODES + n, 8, stride=PART), :] = sum_ref[
                    n * 16 + ea * 8 : n * 16 + ea * 8 + 8, :
                ]
    for e in range(PEERS):
        terms_ref[e * PART + 75 : e * PART + PART, :] = jnp.zeros((PART - 75, LANES), f32)


def stress_kernel(
    f_ref,
    strain_ref,
    moduli_ref,
    sample_high,
    sample_low,
    back_high,
    back_low,
    radius_ref,
    weight_ref,
    forward_ref,
    forward_last_ref,
    adjoint_ref,
    adjoint_last_ref,
    mass_ref,
    forward_out,
    adjoint_out,
    edge_out,
    order_ref,
    moduli_s,
    stress_ref,
    line_ref,
    grid_ref,
):
    for t in range(3):
        for n in range(NODES):
            for ea in range(2):
                order_ref[n * 16 + ea * 8 : n * 16 + ea * 8 + 8, :] = (
                    moduli_ref[pl.ds(ea * 8 * PART + t * NODES + n, 8, stride=PART), :]
                    * float(WEIGHTS[n])
                )
        moduli_s[t] = product(order_ref[...], sample_high[0], sample_low[0])

    @pl.loop(0, NODES)
    def _(n):
        rows = pl.ds(pl.multiple_of(n * 16, 16), 16)
        for side in range(2):
            e = [strain_ref[side, v, rows, :] for v in range(6)]
            for v in range(6):
                total = None
                for w in range(6):
                    r = voigt(v, w)
                    term = (
                        moduli_s[r // 7, rows, (r % 7) * LANES : (r % 7 + 1) * LANES] * e[w]
                    )
                    total = term if total is None else total + term
                stress_ref[side, v, rows, :] = total

    grid_ref[...] = jnp.zeros(grid_ref.shape, f32)

    @pl.loop(0, 2)
    def _(side):
        for ea in range(2):

            def stress(v, i, j):
                return stress_ref[side, v, pl.ds((i * 5 + j) * 16 + ea * 8, 8), :]

            def add(c, turned, i, j, value):
                row, parity = point_rows(ea, i, j)
                at = (2 * parity + turned, side * 3 + c, pl.ds(row, 8, stride=2), slice(None))
                grid_ref[at] = grid_ref[at] + value

            for c, v_a, v_b, v_p in ((0, 0, 5, 4), (1, 5, 1, 3), (2, 4, 3, 2)):
                for j in range(5):
                    line = apply_line(DERIVE.T, [stress(v_a, i, j) for i in range(5)])
                    for i in range(5):
                        line_ref[i * 5 + j] = line[i]
                for i in range(5):
                    line = apply_line(DERIVE.T, [stress(v_b, i, j) for j in range(5)])
                    for j in range(5):
                        add(c, 0, i, j, line_ref[i * 5 + j] + line[j])
                for i in range(5):
                    for j in range(5):
                        at = pl.ds((i * 5 + j) * 16 + ea * 8, 8)
                        add(c, 1, i, j, radius_ref[at, :] * stress(v_p, i, j))

    for c in range(6):
        joined = jnp.concatenate([grid_ref[k, c] for k in range(4)], axis=1)
        force = product(joined, back_high[0], back_low[0])
        edge_out[c] = force[NEXT:ROWS, :]
        now_ref, last_ref, out_ref = (
            (forward_ref, forward_last_ref, forward_out)
            if c < 3
            else (adjoint_ref, adjoint_last_ref, adjoint_out)
        )
        out_ref[c % 3] = (
            2.0 * now_ref[c % 3] - last_ref[c % 3] - mass_ref[...] * force[0:132, :]
        )


def edge_kernel(forward_ref, adjoint_ref, edge_ref, mass_ref, forward_out, adjoint_out):
    forward_out[...] = forward_ref[...] - mass_ref[...] * edge_ref[0:3]
    adjoint_out[...] = adjoint_ref[...] - mass_ref[...] * edge_ref[3:6]


def collect_kernel(terms_ref, out_ref):
    total = terms_ref[0]
    for e in range(1, PEERS):
        total = total + terms_ref[e]
    for t in range(3):
        turned = jnp.transpose(total[t * NODES : t * NODES + NODES, :])
        out_ref[119 * t : 119 * t + 119, :] = turned[0:119, :]


def shape(*dims):
    return jax.ShapeDtypeStruct(dims, f32)


def whole(*dims):
    return pl.BlockSpec(dims, lambda i, f: (0,) * len(dims))


def picked(*dims):
    return pl.BlockSpec((1, *dims), lambda i, f: (f[0],) + (0,) * len(dims))


def kinded(*dims):
    return pl.BlockSpec(
        (1, *dims), lambda i, f: (jnp.minimum(f[0], 1),) + (0,) * len(dims)
    )


def scalars():
    return pl.BlockSpec(memory_space=pltpu.SMEM)


def params(mib):
    return pltpu.CompilerParams(vmem_limit_bytes=mib * 1024 * 1024)


def cost(us):
    return pl.CostEstimate(flops=int(us * 1e6), bytes_accessed=int(us * 3.0e6), transcendentals=0)


def body(forward_now, forward_last, adjoint_now, adjoint_last, moduli, inv_radius, inv_mass):
    f_at = lax.axis_index(FOURIER).astype(jnp.int32).reshape(1)
    slices = lax.axis_size(MERIDIAN)
    wave_high, wave_low = in_two(forward_tables())
    back_high, back_low = in_two(inverse_tables())
    sampling, projection = moduli_tables()
    sample_high, sample_low = in_two(sampling)
    project_high, project_low = in_two(projection)
    weights = jnp.asarray(WEIGHTS, f32)

    first_rows = jnp.concatenate([forward_now[:, :24], adjoint_now[:, :24]], axis=0)
    next_rows = lax.ppermute(first_rows, MERIDIAN, [(s, s - 1) for s in range(1, slices)])

    spread = pl.pallas_call(
        spread_moduli_kernel,
        out_shape=shape(PEERS, PART, LANES),
        compiler_params=params(8),
        cost_estimate=cost(2),
        name="spread",
    )(moduli.reshape(357, NODES))
    gathered = lax.all_to_all(spread, FOURIER, 0, 0, tiled=True).reshape(PEERS * PART, LANES)

    radius = jnp.broadcast_to(
        jnp.transpose(inv_radius.reshape(16, NODES)).reshape(400, 1), (400, LANES)
    )
    mass = jnp.tile(inv_mass.reshape(132, 2), (1, 64))

    x, top, low = pl.pallas_call(
        pack_kernel,
        out_shape=(shape(6, ROWS, LANES), shape(6, CHUNK, LANES), shape(6, CHUNK, LANES)),
        compiler_params=params(8),
        cost_estimate=cost(2),
        name="pack",
    )(forward_now, adjoint_now, next_rows)
    left = lax.ppermute(top, FOURIER, [(i, (i + 1) % PEERS) for i in range(PEERS)])
    right = lax.ppermute(low, FOURIER, [(i, (i - 1) % PEERS) for i in range(PEERS)])

    strain, terms = pl.pallas_call(
        strain_kernel,
        grid_spec=pltpu.PrefetchScalarGridSpec(
            num_scalar_prefetch=1,
            grid=(1,),
            in_specs=[
                whole(6, ROWS, LANES),
                whole(6, CHUNK, LANES),
                whole(6, CHUNK, LANES),
                whole(6, CHUNK, LANES),
                picked(2 * LANES, 4 * LANES),
                picked(2 * LANES, 4 * LANES),
                kinded(7 * LANES, LANES),
                kinded(7 * LANES, LANES),
                whole(400, LANES),
                scalars(),
            ],
            out_specs=(whole(2, 6, 400, LANES), whole(PEERS * PART, LANES)),
            scratch_shapes=[
                pltpu.VMEM((6, ROWS, LANES), f32),
                pltpu.VMEM((3, 3, 4, ROWS, LANES), f32),
                pltpu.VMEM((3, 6, 400, LANES), f32),
                pltpu.VMEM((400, 21 * LANES), bf16),
                pltpu.VMEM((400, 21 * LANES), bf16),
                pltpu.VMEM((400, LANES), f32),
            ],
        ),
        out_shape=(shape(2, 6, 400, LANES), shape(PEERS * PART, LANES)),
        compiler_params=params(40),
        cost_estimate=cost(8),
        name="strain",
    )(
        f_at, x, left, right, top, wave_high, wave_low, project_high, project_low, radius, weights
    )
    arrived = lax.all_to_all(
        terms.reshape(PEERS, PART, LANES), FOURIER, 0, 0, tiled=True
    )

    field = whole(3, 132, LANES)
    forward_part, adjoint_part, edge = pl.pallas_call(
        stress_kernel,
        grid_spec=pltpu.PrefetchScalarGridSpec(
            num_scalar_prefetch=1,
            grid=(1,),
            in_specs=[
                whole(2, 6, 400, LANES),
                whole(PEERS * PART, LANES),
                kinded(LANES, 7 * LANES),
                kinded(LANES, 7 * LANES),
                picked(4 * LANES, LANES),
                picked(4 * LANES, LANES),
                whole(400, LANES),
                scalars(),
                field,
                field,
                field,
                field,
                whole(132, LANES),
            ],
            out_specs=(field, field, whole(6, 24, LANES)),
            scratch_shapes=[
                pltpu.VMEM((400, LANES), f32),
                pltpu.VMEM((3, 400, 7 * LANES), f32),
                pltpu.VMEM((2, 6, 400, LANES), f32),
                pltpu.VMEM((NODES, 8, LANES), f32),
                pltpu.VMEM((4, 6, ROWS, LANES), f32),
            ],
        ),
        out_shape=(shape(3, 132, LANES), shape(3, 132, LANES), shape(6, 24, LANES)),
        compiler_params=params(40),
        cost_estimate=cost(8),
        name="stress",
    )(
        f_at, strain, gathered, sample_high, sample_low, back_high, back_low, radius, weights,
        forward_now, forward_last, adjoint_now, adjoint_last, mass,
    )
    carried = lax.ppermute(edge, MERIDIAN, [(s, s + 1) for s in range(slices - 1)])
    first = pl.BlockSpec((3, 24, LANES), lambda i: (0, 0, 0))
    forward_next, adjoint_next = pl.pallas_call(
        edge_kernel,
        grid=(1,),
        in_specs=[
            first,
            first,
            pl.BlockSpec((6, 24, LANES), lambda i: (0, 0, 0)),
            pl.BlockSpec((24, LANES), lambda i: (0, 0)),
        ],
        out_specs=(first, first),
        out_shape=(shape(3, 132, LANES), shape(3, 132, LANES)),
        input_output_aliases={0: 0, 1: 1},
        compiler_params=params(8),
        name="edge",
    )(forward_part, adjoint_part, carried, mass)
    kernel = pl.pallas_call(
        collect_kernel,
        out_shape=shape(357, NODES),
        compiler_params=params(8),
        name="collect",
    )(arrived)
    return forward_next, adjoint_next, kernel.reshape(21, 17, 1, NODES)


def solution(mesh):
    field = P(None, MERIDIAN, FOURIER)
    moduli = P(None, None, MERIDIAN, FOURIER)
    return jax.shard_map(
        body,
        mesh=mesh,
        in_specs=(field, field, field, field, moduli, P(MERIDIAN), P(MERIDIAN)),
        out_specs=(field, field, moduli),
        check_vma=False,
    )
```

profile of v0, /device:TPU:388, one launch (start us, length us, event | category | flops | bytes accessed | tf_op | source)
XLA Modules:
  0.0 89.4 jit_solution(7098348151392250297)
XLA Ops:
  0.6 0.0 copy-start.21
  0.6 0.0 slice-start.1
  0.7 0.0 copy-start.10
  0.7 0.0 slice-start
  0.7 0.0 copy-start.8
  0.7 0.0 copy-start.22
  0.7 1.5 %reduce = f32[21,17,25]{2,1,0:T(8,128)S(1)} reduce(f32[21,17,1,25]{3,2,1,0:T(1,128)} %param.20, f32[]{:T(128)} %constant.40), dimensions={2}, to_apply=%param.20.reduce_sub_computation | reduce | bytes 71404 | tf_op args[4]
  2.2 1.0 %spread.1 = f32[16,80,128]{2,1,0:T(8,128)} custom-call(f32[357,25]{1,0:T(8,128)S(1)} %reshape.36.moduli_ref), custom_call_target="tpu_custom_call" | custom-call | flops 2000000 | bytes 6000000 | tf_op jit(solution)/shard_map/spread/pallas_call | solution.py:510
  3.2 7.5 %all-to-all-start = ((f32[16,80,128]{2,1,0:T(8,128)}), f32[16,80,128]{2,1,0:T(8,128)S(1)}, u32[]{:S(2)}, u32[]{:S(2)}) async-start(f32[16,80,128]{2,1,0:T(8,128)} %spread.1), calls=%async_computation | async-start | bytes 1310720 | tf_op jit(solution)/shard_map/all_to_all | solution.py:517
  10.6 0.0 slice-done.1
  10.6 0.0 slice-done
  10.7 4.8 %collective-permute-start = (f32[6,24,128]{2,1,0:T(8,128)S(1)}, f32[6,24,128]{2,1,0:T(8,128)S(1)}, u32[]{:S(2)}, u32[]{:S(2)}) collective-permute-start(f32[6,24,128]{2,1,0:T(8,128)S(1)} %pad_maximum_fusion), channel_id=1, source_target_pairs={{1,0},{2,1},{3,2},{4,3},{5,4},{6,5},{7,6},{8,7},{9,8},{10,9},{11,1... | collective-permute-start | bytes 221192 | tf_op jit(solution)/shard_map/ppermute | solution.py:508
  15.4 6.2 %collective-permute-done.next_ref = f32[6,24,128]{2,1,0:T(8,128)S(1)} collective-permute-done((f32[6,24,128]{2,1,0:T(8,128)S(1)}, f32[6,24,128]{2,1,0:T(8,128)S(1)}, u32[]{:S(2)}, u32[]{:S(2)}) %collective-permute-start) | collective-permute-done | bytes 73760 | tf_op jit(solution)/shard_map/ppermute | solution.py:508
  21.6 0.0 copy-done.10
  21.6 0.0 copy-done.8
  21.6 0.3 pack.1
  21.9 0.0 copy-start.13
  21.9 0.8 copy-done.13
  22.7 1.9 %collective-permute-start.1 = (f32[6,40,128]{2,1,0:T(8,128)S(1)}, f32[6,40,128]{2,1,0:T(8,128)S(1)}, u32[]{:S(2)}, u32[]{:S(2)}) collective-permute-start(f32[6,40,128]{2,1,0:T(8,128)S(1)} %get-tuple-element.14.top_ref), channel_id=1, source_target_pairs={{0,32},{32,64},{64,96},{96,128},{128,160},{160,192},{192,224},{224... | collective-permute-start | bytes 368648 | tf_op jit(solution)/shard_map/ppermute | solution.py:531
  24.6 7.3 %collective-permute-start.2 = (f32[6,40,128]{2,1,0:T(8,128)S(1)}, f32[6,40,128]{2,1,0:T(8,128)S(1)}, u32[]{:S(2)}, u32[]{:S(2)}) collective-permute-start(f32[6,40,128]{2,1,0:T(8,128)S(1)} %get-tuple-element.15), channel_id=1, source_target_pairs={{0,480},{32,0},{64,32},{96,64},{128,96},{160,128},{192,160},{224,1... | collective-permute-start | bytes 368648 | tf_op jit(solution)/shard_map/ppermute | solution.py:532
  31.9 0.0 copy-done.22
  31.9 0.1 reshape.31
  32.0 0.1 copy.29
  32.1 0.1 broadcast_in_dim.7
  32.1 0.3 collective-permute-done.1.left_ref
  32.5 1.8 %collective-permute-done.2.right_ref = f32[6,40,128]{2,1,0:T(8,128)S(1)} collective-permute-done((f32[6,40,128]{2,1,0:T(8,128)S(1)}, f32[6,40,128]{2,1,0:T(8,128)S(1)}, u32[]{:S(2)}, u32[]{:S(2)}) %collective-permute-start.2) | collective-permute-done | bytes 122912 | tf_op jit(solution)/shard_map/ppermute | solution.py:532
  34.3 0.1 broadcast_in_dim.8.radius_ref
  34.4 0.0 copy-done.21
  34.4 0.0 copy-start
  34.4 2.2 %copy-done = bf16[16,256,512]{2,1,0:T(8,128)(2,1)S(1)} copy-done((bf16[16,256,512]{2,1,0:T(8,128)(2,1)S(1)}, bf16[16,256,512]{2,1,0:T(8,128)(2,1)}, u32[]{:S(2)}) %copy-start) | copy-done | bytes 4194328
  36.6 2.2 %copy-done.1 = bf16[16,256,512]{2,1,0:T(8,128)(2,1)S(1)} copy-done((bf16[16,256,512]{2,1,0:T(8,128)(2,1)S(1)}, bf16[16,256,512]{2,1,0:T(8,128)(2,1)}, u32[]{:S(2)}) %copy-start.1) | copy-done | bytes 4194328
  38.8 1.0 %copy-done.14 = f32[6,160,128]{2,1,0:T(8,128)S(1)} copy-done((f32[6,160,128]{2,1,0:T(8,128)S(1)}, f32[6,160,128]{2,1,0:T(8,128)}, u32[]{:S(2)}) %copy-start.14) | copy-done | bytes 491544
  39.8 1.0 %copy-done.17 = bf16[2,896,128]{2,1,0:T(8,128)(2,1)S(1)} copy-done((bf16[2,896,128]{2,1,0:T(8,128)(2,1)S(1)}, bf16[2,896,128]{2,1,0:T(8,128)(2,1)}, u32[]{:S(2)}) %copy-start.17) | copy-done | bytes 458776
  40.8 1.0 %copy-done.18 = bf16[2,896,128]{2,1,0:T(8,128)(2,1)S(1)} copy-done((bf16[2,896,128]{2,1,0:T(8,128)(2,1)S(1)}, bf16[2,896,128]{2,1,0:T(8,128)(2,1)}, u32[]{:S(2)}) %copy-start.18) | copy-done | bytes 458776
  41.9 6.7 %strain.1 = (f32[2,6,400,128]{3,2,1,0:T(8,128)S(1)}, f32[1280,128]{1,0:T(8,128)S(1)}) custom-call(s32[1]{0:T(128)} %bitcast.f_ref, f32[6,160,128]{2,1,0:T(8,128)S(1)} %copy-done.14, f32[6,40,128]{2,1,0:T(8,128)S(1)} %collective-permute-done.1.left_ref, f32[6,40,128]{2,1,0:T(8,128)S(1)} %collective-permute-done.2.right_ref, ...), custom_call_target="tpu_custom_call" | custom-call | flops 8000000 | bytes 24000000 | tf_op jit(solution)/shard_map/strain/pallas_call | solution.py:534
  48.5 0.0 copy-start.2
  48.5 1.5 %copy-done.2 = f32[2,6,400,128]{3,2,1,0:T(8,128)} copy-done((f32[2,6,400,128]{3,2,1,0:T(8,128)}, f32[2,6,400,128]{3,2,1,0:T(8,128)S(1)}, u32[]{:S(2)}) %copy-start.2) | copy-done | bytes 2457624
  50.0 0.7 copy-done.6
  50.7 0.8 copy-done.12
  51.5 0.0 all-to-all-done
  51.5 7.3 %all-to-all-start.1 = ((f32[16,80,128]{2,1,0:T(8,128)}), f32[16,80,128]{2,1,0:T(8,128)S(1)}, u32[]{:S(2)}, u32[]{:S(2)}) async-start(f32[16,80,128]{2,1,0:T(8,128)} %bitcast.7), calls=%async_computation.1 | async-start | bytes 1310720 | tf_op jit(solution)/shard_map/all_to_all | solution.py:568
  58.9 0.0 copy-done.23
  58.9 0.1 tile.10
  59.0 0.1 copy.32
  59.1 0.7 tile.11
  59.8 1.6 %tile.12 = f32[132,128]{0,1:T(8,128)} reshape(f32[132,64,2]{0,2,1:T(2,128)} %tile.11) | data formatting | bytes 135168 | tf_op jit(solution)/shard_map/tile | solution.py:522
  61.4 1.0 %copy.33.mass_ref = f32[132,128]{1,0:T(8,128)S(1)} copy(f32[132,128]{0,1:T(8,128)} %tile.12) | data formatting | bytes 135168 | tf_op jit(solution)/shard_map/tile | solution.py:522
  62.4 0.0 copy-done.4
  62.4 1.7 %copy-done.3 = f32[2,6,400,128]{3,2,1,0:T(8,128)S(1)} copy-done((f32[2,6,400,128]{3,2,1,0:T(8,128)S(1)}, f32[2,6,400,128]{3,2,1,0:T(8,128)}, u32[]{:S(2)}) %copy-start.3) | copy-done | bytes 2457624
  64.1 1.6 %copy-done.5 = bf16[16,512,128]{2,1,0:T(8,128)(2,1)S(1)} copy-done((bf16[16,512,128]{2,1,0:T(8,128)(2,1)S(1)}, bf16[16,512,128]{2,1,0:T(8,128)(2,1)}, u32[]{:S(2)}) %copy-start.5) | copy-done | bytes 2097176
  65.7 0.9 %copy-done.7 = f32[400,128]{1,0:T(8,128)S(1)} copy-done((f32[400,128]{1,0:T(8,128)S(1)}, f32[400,128]{1,0:T(8,128)}, u32[]{:S(2)}) %copy-start.7) | copy-done | bytes 204824
  66.7 0.9 %copy-done.9 = f32[3,132,128]{2,1,0:T(8,128)S(1)} copy-done((f32[3,132,128]{2,1,0:T(8,128)S(1)}, f32[3,132,128]{2,1,0:T(8,128)}, u32[]{:S(2)}) %copy-start.9) | copy-done | bytes 202776
  67.6 0.9 %copy-done.11 = f32[3,132,128]{2,1,0:T(8,128)S(1)} copy-done((f32[3,132,128]{2,1,0:T(8,128)S(1)}, f32[3,132,128]{2,1,0:T(8,128)}, u32[]{:S(2)}) %copy-start.11) | copy-done | bytes 202776
  68.5 1.0 %copy-done.15 = bf16[2,128,896]{2,1,0:T(8,128)(2,1)S(1)} copy-done((bf16[2,128,896]{2,1,0:T(8,128)(2,1)S(1)}, bf16[2,128,896]{2,1,0:T(8,128)(2,1)}, u32[]{:S(2)}) %copy-start.15) | copy-done | bytes 458776
  69.5 1.0 %copy-done.16 = bf16[2,128,896]{2,1,0:T(8,128)(2,1)S(1)} copy-done((bf16[2,128,896]{2,1,0:T(8,128)(2,1)S(1)}, bf16[2,128,896]{2,1,0:T(8,128)(2,1)}, u32[]{:S(2)}) %copy-start.16) | copy-done | bytes 458776
  70.6 0.9 %copy-done.19 = f32[3,132,128]{2,1,0:T(8,128)S(1)} copy-done((f32[3,132,128]{2,1,0:T(8,128)S(1)}, f32[3,132,128]{2,1,0:T(8,128)}, u32[]{:S(2)}) %copy-start.19) | copy-done | bytes 202776
  71.5 0.9 %copy-done.20 = f32[3,132,128]{2,1,0:T(8,128)S(1)} copy-done((f32[3,132,128]{2,1,0:T(8,128)S(1)}, f32[3,132,128]{2,1,0:T(8,128)}, u32[]{:S(2)}) %copy-start.20) | copy-done | bytes 202776
  72.4 6.2 %stress.1 = (f32[3,132,128]{2,1,0:T(8,128)}, f32[3,132,128]{2,1,0:T(8,128)}, f32[6,24,128]{2,1,0:T(8,128)S(1)}) custom-call(s32[1]{0:T(128)} %bitcast.f_ref, f32[2,6,400,128]{3,2,1,0:T(8,128)S(1)} %copy-done.3, f32[1280,128]{1,0:T(8,128)S(1)} %bitcast.6, bf16[2,128,896]{2,1,0:T(8,128)(2,1)S(1)} %copy-done.15, bf16[2,128,896]{2,1,0:T(8,128)(2,1)S(1)} %copy-done.16, ...), custom_call_target="tpu_custom_call" | custom-call | flops 8000000 | bytes 24000000 | tf_op jit(solution)/shard_map/stress/pallas_call | solution.py:573
  78.6 1.9 %collective-permute-start.3 = (f32[6,24,128]{2,1,0:T(8,128)S(1)}, f32[6,24,128]{2,1,0:T(8,128)S(1)}, u32[]{:S(2)}, u32[]{:S(2)}) collective-permute-start(f32[6,24,128]{2,1,0:T(8,128)S(1)} %get-tuple-element.19), channel_id=1, source_target_pairs={{0,1},{1,2},{2,3},{3,4},{4,5},{5,6},{6,7},{7,8},{8,9},{9,10},{10,1... | collective-permute-start | bytes 221192 | tf_op jit(solution)/shard_map/ppermute | solution.py:610
  80.5 6.4 %collective-permute-done.3.edge_ref = f32[6,24,128]{2,1,0:T(8,128)S(1)} collective-permute-done((f32[6,24,128]{2,1,0:T(8,128)S(1)}, f32[6,24,128]{2,1,0:T(8,128)S(1)}, u32[]{:S(2)}, u32[]{:S(2)}) %collective-permute-start.3) | collective-permute-done | bytes 73760 | tf_op jit(solution)/shard_map/ppermute | solution.py:610
  86.9 1.4 %edge.1 = (f32[3,132,128]{2,1,0:T(8,128)}, f32[3,132,128]{2,1,0:T(8,128)}) custom-call(f32[3,132,128]{2,1,0:T(8,128)} %get-tuple-element.17.forward_ref, f32[3,132,128]{2,1,0:T(8,128)} %get-tuple-element.18.adjoint_ref, f32[6,24,128]{2,1,0:T(8,128)S(1)} %collective-permute-done.3.edge_ref, ...), custom_call_target="tpu_custom_call", output_to_operand_aliasing={{0}: (0, {}), {1}: (1, {})} | custom-call | tf_op jit(solution)/shard_map/edge/pallas_call | solution.py:612
  88.4 0.0 all-to-all-done.1.terms_ref
  88.4 0.1 collect.1
  88.5 0.9 reshape.38
  (19 shorter events, 0.1 us)
Async XLA Ops:
  0.6 33.8 %copy-start.21 = (f32[25]{0:T(128)S(1)}, f32[25]{0:T(128)}, u32[]{:S(2)}) copy-start(f32[25]{0:T(128)} %constant.24.clone.weight_ref) | copy-start | bytes 304
  0.6 10.0 %slice-start.1 = ((f32[3,132,128]{2,1,0:T(8,128)}), f32[3,24,128]{2,1,0:T(8,128)S(1)}, s32[]{:S(2)}) async-start(f32[3,132,128]{2,1,0:T(8,128)} %adjoint_ref.3), calls=%async_computation.3 | async-start | bytes 73728 | tf_op jit(solution)/shard_map/slice | solution.py:507
  0.7 21.0 %copy-start.10 = (f32[3,132,128]{2,1,0:T(8,128)S(1)}, f32[3,132,128]{2,1,0:T(8,128)}, u32[]{:S(2)}) copy-start(f32[3,132,128]{2,1,0:T(8,128)} %adjoint_ref.3) | copy-start | bytes 608260
  0.7 10.0 %slice-start = ((f32[3,132,128]{2,1,0:T(8,128)}), f32[3,24,128]{2,1,0:T(8,128)S(1)}, s32[]{:S(2)}) async-start(f32[3,132,128]{2,1,0:T(8,128)} %forward_ref.3), calls=%async_computation.2 | async-start | bytes 73728 | tf_op jit(solution)/shard_map/slice | solution.py:507
  0.7 21.0 %copy-start.8 = (f32[3,132,128]{2,1,0:T(8,128)S(1)}, f32[3,132,128]{2,1,0:T(8,128)}, u32[]{:S(2)}) copy-start(f32[3,132,128]{2,1,0:T(8,128)} %forward_ref.3) | copy-start | bytes 608260
  0.7 31.2 %copy-start.22 = (f32[400]{0:T(512)S(1)}, f32[400]{0:T(512)}, u32[]{:S(2)}) copy-start(f32[400]{0:T(512)} %param.21) | copy-start | bytes 4804
  3.2 48.3 %all-to-all-start = ((f32[16,80,128]{2,1,0:T(8,128)}), f32[16,80,128]{2,1,0:T(8,128)S(1)}, u32[]{:S(2)}, u32[]{:S(2)}) async-start(f32[16,80,128]{2,1,0:T(8,128)} %spread.1), calls=%async_computation | async-start | bytes 1310720 | tf_op jit(solution)/shard_map/all_to_all | solution.py:517
  10.7 11.0 %collective-permute-start = (f32[6,24,128]{2,1,0:T(8,128)S(1)}, f32[6,24,128]{2,1,0:T(8,128)S(1)}, u32[]{:S(2)}, u32[]{:S(2)}) collective-permute-start(f32[6,24,128]{2,1,0:T(8,128)S(1)} %pad_maximum_fusion), channel_id=1, source_target_pairs={{1,0},{2,1},{3,2},{4,3},{5,4},{6,5},{7,6},{8,7},{9,8},{10,9},{11,1... | collective-permute-start | bytes 221192 | tf_op jit(solution)/shard_map/ppermute | solution.py:508
  21.9 0.8 copy-start.13
  22.7 9.8 %collective-permute-start.1 = (f32[6,40,128]{2,1,0:T(8,128)S(1)}, f32[6,40,128]{2,1,0:T(8,128)S(1)}, u32[]{:S(2)}, u32[]{:S(2)}) collective-permute-start(f32[6,40,128]{2,1,0:T(8,128)S(1)} %get-tuple-element.14.top_ref), channel_id=1, source_target_pairs={{0,32},{32,64},{64,96},{96,128},{128,160},{160,192},{192,224},{224... | collective-permute-start | bytes 368648 | tf_op jit(solution)/shard_map/ppermute | solution.py:531
  24.6 9.7 %collective-permute-start.2 = (f32[6,40,128]{2,1,0:T(8,128)S(1)}, f32[6,40,128]{2,1,0:T(8,128)S(1)}, u32[]{:S(2)}, u32[]{:S(2)}) collective-permute-start(f32[6,40,128]{2,1,0:T(8,128)S(1)} %get-tuple-element.15), channel_id=1, source_target_pairs={{0,480},{32,0},{64,32},{96,64},{128,96},{160,128},{192,160},{224,1... | collective-permute-start | bytes 368648 | tf_op jit(solution)/shard_map/ppermute | solution.py:532
  34.4 2.2 %copy-start = (bf16[16,256,512]{2,1,0:T(8,128)(2,1)S(1)}, bf16[16,256,512]{2,1,0:T(8,128)(2,1)}, u32[]{:S(2)}) copy-start(bf16[16,256,512]{2,1,0:T(8,128)(2,1)} %constant.25.clone.wave_high) | copy-start | bytes 12582916
  36.6 2.2 %copy-start.1 = (bf16[16,256,512]{2,1,0:T(8,128)(2,1)S(1)}, bf16[16,256,512]{2,1,0:T(8,128)(2,1)}, u32[]{:S(2)}) copy-start(bf16[16,256,512]{2,1,0:T(8,128)(2,1)} %constant.26.clone.wave_low) | copy-start | bytes 12582916
  38.8 1.0 %copy-start.14 = (f32[6,160,128]{2,1,0:T(8,128)S(1)}, f32[6,160,128]{2,1,0:T(8,128)}, u32[]{:S(2)}) copy-start(f32[6,160,128]{2,1,0:T(8,128)} %copy-done.13) | copy-start | bytes 1474564
  39.8 1.0 %copy-start.17 = (bf16[2,896,128]{2,1,0:T(8,128)(2,1)S(1)}, bf16[2,896,128]{2,1,0:T(8,128)(2,1)}, u32[]{:S(2)}) copy-start(bf16[2,896,128]{2,1,0:T(8,128)(2,1)} %constant.27.clone.project_high) | copy-start | bytes 1376260
  40.8 1.0 %copy-start.18 = (bf16[2,896,128]{2,1,0:T(8,128)(2,1)S(1)}, bf16[2,896,128]{2,1,0:T(8,128)(2,1)}, u32[]{:S(2)}) copy-start(bf16[2,896,128]{2,1,0:T(8,128)(2,1)} %constant.28.clone.project_low) | copy-start | bytes 1376260
  41.9 17.0 %copy-start.23 = (f32[264]{0:T(512)S(1)}, f32[264]{0:T(512)}, u32[]{:S(2)}) copy-start(f32[264]{0:T(512)} %param.22) | copy-start | bytes 3172
  41.9 20.6 %copy-start.4 = (bf16[16,512,128]{2,1,0:T(8,128)(2,1)S(1)}, bf16[16,512,128]{2,1,0:T(8,128)(2,1)}, u32[]{:S(2)}) copy-start(bf16[16,512,128]{2,1,0:T(8,128)(2,1)} %constant.31.clone.back_high) | copy-start | bytes 6291460
  48.5 1.5 %copy-start.2 = (f32[2,6,400,128]{3,2,1,0:T(8,128)}, f32[2,6,400,128]{3,2,1,0:T(8,128)S(1)}, u32[]{:S(2)}) copy-start(f32[2,6,400,128]{3,2,1,0:T(8,128)S(1)} %get-tuple-element.16.strain_ref) | copy-start | bytes 7372804
  50.0 0.7 copy-start.6
  50.7 0.8 copy-start.12
  51.5 36.9 %all-to-all-start.1 = ((f32[16,80,128]{2,1,0:T(8,128)}), f32[16,80,128]{2,1,0:T(8,128)S(1)}, u32[]{:S(2)}, u32[]{:S(2)}) async-start(f32[16,80,128]{2,1,0:T(8,128)} %bitcast.7), calls=%async_computation.1 | async-start | bytes 1310720 | tf_op jit(solution)/shard_map/all_to_all | solution.py:568
  62.4 1.7 %copy-start.3 = (f32[2,6,400,128]{3,2,1,0:T(8,128)S(1)}, f32[2,6,400,128]{3,2,1,0:T(8,128)}, u32[]{:S(2)}) copy-start(f32[2,6,400,128]{3,2,1,0:T(8,128)} %copy-done.2) | copy-start | bytes 7372804
  64.1 1.6 %copy-start.5 = (bf16[16,512,128]{2,1,0:T(8,128)(2,1)S(1)}, bf16[16,512,128]{2,1,0:T(8,128)(2,1)}, u32[]{:S(2)}) copy-start(bf16[16,512,128]{2,1,0:T(8,128)(2,1)} %constant.32.clone.back_low) | copy-start | bytes 6291460
  65.7 0.9 %copy-start.7 = (f32[400,128]{1,0:T(8,128)S(1)}, f32[400,128]{1,0:T(8,128)}, u32[]{:S(2)}) copy-start(f32[400,128]{1,0:T(8,128)} %copy-done.6) | copy-start | bytes 614404
  66.7 0.9 %copy-start.9 = (f32[3,132,128]{2,1,0:T(8,128)S(1)}, f32[3,132,128]{2,1,0:T(8,128)}, u32[]{:S(2)}) copy-start(f32[3,132,128]{2,1,0:T(8,128)} %forward_ref.3) | copy-start | bytes 608260
  67.6 0.9 %copy-start.11 = (f32[3,132,128]{2,1,0:T(8,128)S(1)}, f32[3,132,128]{2,1,0:T(8,128)}, u32[]{:S(2)}) copy-start(f32[3,132,128]{2,1,0:T(8,128)} %adjoint_ref.3) | copy-start | bytes 608260
  68.5 1.0 %copy-start.15 = (bf16[2,128,896]{2,1,0:T(8,128)(2,1)S(1)}, bf16[2,128,896]{2,1,0:T(8,128)(2,1)}, u32[]{:S(2)}) copy-start(bf16[2,128,896]{2,1,0:T(8,128)(2,1)} %constant.29.clone.sample_high) | copy-start | bytes 1376260
  69.5 1.0 %copy-start.16 = (bf16[2,128,896]{2,1,0:T(8,128)(2,1)S(1)}, bf16[2,128,896]{2,1,0:T(8,128)(2,1)}, u32[]{:S(2)}) copy-start(bf16[2,128,896]{2,1,0:T(8,128)(2,1)} %constant.30.clone.sample_low) | copy-start | bytes 1376260
  70.6 0.9 %copy-start.19 = (f32[3,132,128]{2,1,0:T(8,128)S(1)}, f32[3,132,128]{2,1,0:T(8,128)}, u32[]{:S(2)}) copy-start(f32[3,132,128]{2,1,0:T(8,128)} %forward_last_ref.1) | copy-start | bytes 608260
  71.5 0.9 %copy-start.20 = (f32[3,132,128]{2,1,0:T(8,128)S(1)}, f32[3,132,128]{2,1,0:T(8,128)}, u32[]{:S(2)}) copy-start(f32[3,132,128]{2,1,0:T(8,128)} %adjoint_last_ref.1) | copy-start | bytes 608260
  78.6 8.3 %collective-permute-start.3 = (f32[6,24,128]{2,1,0:T(8,128)S(1)}, f32[6,24,128]{2,1,0:T(8,128)S(1)}, u32[]{:S(2)}, u32[]{:S(2)}) collective-permute-start(f32[6,24,128]{2,1,0:T(8,128)S(1)} %get-tuple-element.19), channel_id=1, source_target_pairs={{0,1},{1,2},{2,3},{3,4},{4,5},{5,6},{6,7},{7,8},{8,9},{9,10},{10,1... | collective-permute-start | bytes 221192 | tf_op jit(solution)/shard_map/ppermute | solution.py:610
where the time goes:
time: 90.4 us; the launch traced here: 89.4 us
  starting transfers between devices  30.6 us (34%)
  local copies, waits for them, and re-layouts  26 us (29%)
  Pallas kernels  15.6 us (17%)
  waiting for transfers between devices  14.8 us (16%)
  other arithmetic  1.5 us (2%)
    unnamed x48, local copies, waits for them, and re-layouts  21.2 us
    all_to_all x1, starting transfers between devices, body(): lax.all_to_all(spread, FOURIER, 0, 0, tiled=True)  7.45 us
    all_to_all x1, starting transfers between devices, body(): lax.all_to_all(terms.reshape(PEERS, PART, LANES), FOURIER, 0, 0, tiled=True)  7.33 us
    ppermute x1, starting transfers between devices, body(): lax.ppermute(low, FOURIER, [(i, (i - 1) % PEERS) for i in range(PEERS)])  7.26 us
    pallas_call x1, Pallas kernels, body(): pl.pallas_call(strain_kernel, grid_spec=pltpu.PrefetchScalarGridSpec(num_...  6.66 us
    ppermute x1, waiting for transfers between devices, body(): lax.ppermute(edge, MERIDIAN, [(s, s + 1) for s in range(slices - 1)])  6.43 us
    ppermute x1, waiting for transfers between devices, body(): lax.ppermute(first_rows, MERIDIAN, [(s, s - 1) for s in range(1, slices)])  6.2 us
    pallas_call x1, Pallas kernels, body(): pl.pallas_call(stress_kernel, grid_spec=pltpu.PrefetchScalarGridSpec(num_...  6.18 us
  transfers between devices with their start and end apart: 6, of which 4 were waited for; matrix products, arithmetic and copies ran while one was open for 4% of the time, Pallas kernels for 16%

commit v1 on v0

--- a/solution.py
+++ b/solution.py
@@ -21,6 +21,7 @@
 CHUNK = 40
 PART = 80
 NODES = 25
+LIMIT = 50 * 1024 * 1024
 
 f32 = jnp.float32
 bf16 = jnp.bfloat16
@@ -157,6 +158,26 @@
     return high, low
 
 
+BACK_ROWS = 2 * 4 * LANES
+KIND_ROWS = 2 * 7 * LANES
+PROJECT_AT = PEERS * BACK_ROWS
+SAMPLE_AT = PROJECT_AT + 2 * KIND_ROWS
+
+
+def narrow_tables():
+    sampling, projection = moduli_tables()
+    blocks = np.stack(np.split(sampling, 7, axis=2), axis=1)
+    parts = [
+        np.stack(in_two(table), axis=1).reshape(-1, LANES)
+        for table in (inverse_tables(), projection, blocks)
+    ]
+    return np.concatenate(parts)
+
+
+def table_rows(table_hbm, at, count):
+    return table_hbm.at[pl.ds(pl.multiple_of(at, LANES), count), :]
+
+
 def gll():
     x = np.array([-1.0, -math.sqrt(3.0 / 7.0), 0.0, math.sqrt(3.0 / 7.0), 1.0])
     weights = np.array([0.1, 49.0 / 90.0, 32.0 / 45.0, 49.0 / 90.0, 0.1])
@@ -218,22 +239,38 @@
     return at // 2, at % 2
 
 
-def spread_moduli_kernel(moduli_ref, out_ref):
+def started(sems, pairs):
+    copies = [pltpu.make_async_copy(a, b, sems.at[n]) for n, (a, b) in enumerate(pairs)]
+    for copy in copies:
+        copy.start()
+    return copies
+
+
+def spread_kernel(moduli_hbm, spread_hbm, moduli_ref, part_ref, sems, out_sems):
+    (moduli_copy,) = started(sems, ((moduli_hbm, moduli_ref),))
+    part_ref[72:PART, :] = jnp.zeros((PART - 72, LANES), f32)
+    moduli_copy.wait()
     for t in range(3):
-        block = moduli_ref[119 * t : 119 * t + 119, :]
-        block = jnp.concatenate([block, jnp.zeros((LANES - 119, NODES), f32)], axis=0)
-        turned = jnp.transpose(block)
-        for e in range(PEERS):
-            out_ref[e, t * NODES : t * NODES + NODES, :] = turned
-    for e in range(PEERS):
-        out_ref[e, 75:PART, :] = jnp.zeros((PART - 75, LANES), f32)
-
-
-def pack_kernel(forward_ref, adjoint_ref, next_ref, x_ref, top_ref, low_ref):
-    x_ref[0:3, 0:132, :] = forward_ref[...]
-    x_ref[3:6, 0:132, :] = adjoint_ref[...]
+        rows = [moduli_ref[7 * t + r, :, 0, :] for r in range(7)]
+        block = jnp.concatenate(rows + [jnp.zeros((LANES - 119, NODES), f32)], axis=0)
+        part_ref[t * NODES : t * NODES + NODES, :] = jnp.transpose(block)
+    for copy in started(out_sems, [(part_ref, spread_hbm.at[e]) for e in range(PEERS)]):
+        copy.wait()
+
+
+def pack_kernel(
+    now_hbm, next_hbm, far_hbm, near_hbm, top_hbm, x_ref, top_ref, low_ref, sems, out_sems
+):
+    copies = started(
+        sems,
+        (
+            (now_hbm, x_ref.at[:, 0:132, :]),
+            (next_hbm, x_ref.at[:, NEXT:ROWS, :]),
+        ),
+    )
     x_ref[:, 132:NEXT, :] = jnp.zeros((6, NEXT - 132, LANES), f32)
-    x_ref[:, NEXT:ROWS, :] = next_ref[...]
+    for copy in copies:
+        copy.wait()
     group = lax.broadcasted_iota(jnp.int32, (CHUNK, LANES), 1) // 32
     for c in range(6):
         low = x_ref[c, 0:CHUNK, :]
@@ -246,52 +283,101 @@
             )
         low_ref[c] = low
         top_ref[c] = top
+    odd = lax.rem(lax.axis_index(FOURIER), 2)
+    (top_copy,) = started(out_sems, ((top_ref, top_hbm),))
+
+    @pl.when(odd == 0)
+    def _():
+        far = pltpu.make_async_copy(low_ref, far_hbm, out_sems.at[1])
+        near = pltpu.make_async_copy(top_ref, near_hbm, out_sems.at[2])
+        far.start()
+        near.start()
+        far.wait()
+        near.wait()
+
+    @pl.when(odd == 1)
+    def _():
+        far = pltpu.make_async_copy(top_ref, far_hbm, out_sems.at[1])
+        near = pltpu.make_async_copy(low_ref, near_hbm, out_sems.at[2])
+        far.start()
+        near.start()
+        far.wait()
+        near.wait()
+
+    top_copy.wait()
 
 
 def strain_kernel(
-    f_ref,
+    now_hbm,
+    next_hbm,
+    far_hbm,
+    near_hbm,
+    top_hbm,
+    wave_hbm,
+    table_hbm,
+    radius_hbm,
+    strain_hbm,
+    terms_hbm,
     x_ref,
-    left_ref,
-    right_ref,
+    beside_ref,
     top_ref,
-    wave_high,
-    wave_low,
-    project_high,
-    project_low,
+    wave,
+    project,
     radius_ref,
-    weight_ref,
     strain_ref,
-    terms_ref,
     halo_ref,
     sample_ref,
     central_ref,
     high_ref,
     low_ref,
     sum_ref,
+    terms_ref,
+    sems,
+    out_sems,
 ):
+    f_at = lax.axis_index(FOURIER)
+    copies = started(
+        sems,
+        (
+            (far_hbm, beside_ref.at[lax.rem(f_at, 2)]),
+            (near_hbm, beside_ref.at[1 - lax.rem(f_at, 2)]),
+            (top_hbm, top_ref),
+            (wave_hbm.at[f_at], wave),
+            (now_hbm, x_ref.at[:, 0:132, :]),
+            (next_hbm, x_ref.at[:, NEXT:ROWS, :]),
+            (radius_hbm, radius_ref),
+            (
+                table_rows(table_hbm, PROJECT_AT + KIND_ROWS * jnp.minimum(f_at, 1), KIND_ROWS),
+                project,
+            ),
+        ),
+    )
+    x_ref[:, 132:NEXT, :] = jnp.zeros((6, NEXT - 132, LANES), f32)
+    for copy in copies[:3]:
+        copy.wait()
     group = lax.broadcasted_iota(jnp.int32, (CHUNK, LANES), 1) // 32
     for c in range(6):
-        left, right, top = left_ref[c], right_ref[c], top_ref[c]
+        left, right, top = beside_ref[0, c], beside_ref[1, c], top_ref[c]
         for g in range(4):
             a = left if g == 0 else pltpu.roll(left, (-32 * g) % LANES, 1)
             b = right if g == 1 else pltpu.roll(right, (32 - 32 * g) % LANES, 1)
             d = top if g == 2 else pltpu.roll(top, (64 - 32 * g) % LANES, 1)
             rows = jnp.where(group == 0, a, jnp.where(group == 1, b, d))
             halo_ref[c, CHUNK * g : CHUNK * g + CHUNK, :] = jnp.where(group == 3, 0.0, rows)
+    for copy in copies[3:7]:
+        copy.wait()
+    radius_copy = pltpu.make_async_copy(radius_ref, strain_hbm.at[12], out_sems.at[2])
+    radius_copy.start()
     for c in range(6):
-        own = product(x_ref[c], wave_high[0, :LANES, :], wave_low[0, :LANES, :])
-        beside = product(halo_ref[c], wave_high[0, LANES:, :], wave_low[0, LANES:, :])
+        own = product(x_ref[c], wave[0, :LANES, :], wave[1, :LANES, :])
+        beside = product(halo_ref[c], wave[0, LANES:, :], wave[1, LANES:, :])
         both = own + beside
         for k in range(4):
             sample_ref[c // 3, c % 3, k] = both[:, k * LANES : (k + 1) * LANES]
             if c < 3:
                 sample_ref[2, c, k] = own[:, k * LANES : (k + 1) * LANES]
 
-    @pl.loop(0, 3)
-    def _(which):
-        def strain_of(v):
-            return strain_ref.at[which, v]
-
+    def strains(which, out_ref, out_at):
         for ea in range(2):
 
             def node(c, turned, i, j):
@@ -302,10 +388,10 @@
                 return pl.ds((i * 5 + j) * 16 + ea * 8, 8)
 
             def store(v, i, j, value, add):
-                at = (which, v, place(i, j), slice(None))
+                at = (out_at + v, place(i, j), slice(None))
                 if add:
-                    value = value + central_ref[at]
-                central_ref[at] = value
+                    value = value + out_ref[at]
+                out_ref[at] = value
 
             for c, v_a, v_b, v_p, add_a, add_b in (
                 (0, 0, 5, 4, False, False),
@@ -326,13 +412,19 @@
                     for j in range(5):
                         store(v_b, i, j, line[j], add_b)
 
-    strain_ref[...] = central_ref[0:2]
+    @pl.loop(0, 2)
+    def _(which):
+        strains(which, strain_ref, which * 6)
+
+    strain_copy = pltpu.make_async_copy(strain_ref, strain_hbm.at[0:12], out_sems.at[0])
+    strain_copy.start()
+    strains(2, central_ref, 0)
 
     @pl.loop(0, NODES)
     def _(n):
         rows = pl.ds(pl.multiple_of(n * 16, 16), 16)
-        a = [central_ref[1, v, rows, :] for v in range(6)]
-        f = [central_ref[2, v, rows, :] * weight_ref[n] for v in range(6)]
+        a = [strain_ref[6 + v, rows, :] for v in range(6)]
+        f = [central_ref[v, rows, :] for v in range(6)]
         for v in range(6):
             for w in range(v, 6):
                 term = f[v] * a[w]
@@ -343,47 +435,79 @@
                 high_ref[rows, r * LANES : (r + 1) * LANES] = high
                 low_ref[rows, r * LANES : (r + 1) * LANES] = low
 
+    copies[7].wait()
     for t in range(3):
         cut = slice(t * 7 * LANES, (t + 1) * 7 * LANES)
         high, low = high_ref[:, cut], low_ref[:, cut]
         sum_ref[...] = (
-            jnp.dot(high, project_high[0], preferred_element_type=f32)
-            + jnp.dot(low, project_high[0], preferred_element_type=f32)
-            + jnp.dot(high, project_low[0], preferred_element_type=f32)
+            jnp.dot(high, project[: 7 * LANES, :], preferred_element_type=f32)
+            + jnp.dot(low, project[: 7 * LANES, :], preferred_element_type=f32)
+            + jnp.dot(high, project[7 * LANES :, :], preferred_element_type=f32)
         )
         for n in range(NODES):
             for ea in range(2):
                 terms_ref[pl.ds(ea * 8 * PART + t * NODES + n, 8, stride=PART), :] = sum_ref[
                     n * 16 + ea * 8 : n * 16 + ea * 8 + 8, :
-                ]
+                ] * float(WEIGHTS[n])
     for e in range(PEERS):
         terms_ref[e * PART + 75 : e * PART + PART, :] = jnp.zeros((PART - 75, LANES), f32)
+    terms_copy = pltpu.make_async_copy(terms_ref, terms_hbm, out_sems.at[1])
+    terms_copy.start()
+    strain_copy.wait()
+    radius_copy.wait()
+    terms_copy.wait()
 
 
 def stress_kernel(
-    f_ref,
-    strain_ref,
-    moduli_ref,
-    sample_high,
-    sample_low,
-    back_high,
-    back_low,
-    radius_ref,
-    weight_ref,
-    forward_ref,
-    forward_last_ref,
-    adjoint_ref,
-    adjoint_last_ref,
-    mass_ref,
+    moduli_hbm,
+    table_hbm,
+    strain_hbm,
+    forward_hbm,
+    adjoint_hbm,
+    forward_last_hbm,
+    adjoint_last_hbm,
+    mass_hbm,
     forward_out,
     adjoint_out,
-    edge_out,
+    edge_hbm,
+    moduli_ref,
+    sample,
+    strain_ref,
+    back,
+    now_ref,
+    last_ref,
+    mass_ref,
+    out_ref,
+    edge_ref,
     order_ref,
     moduli_s,
     stress_ref,
     line_ref,
     grid_ref,
+    sems,
+    out_sems,
 ):
+    f_at = lax.axis_index(FOURIER)
+    copies = started(
+        sems,
+        (
+            (moduli_hbm, moduli_ref),
+            (
+                table_rows(table_hbm, SAMPLE_AT + KIND_ROWS * jnp.minimum(f_at, 1), KIND_ROWS),
+                sample,
+            ),
+            (strain_hbm, strain_ref),
+            (table_rows(table_hbm, BACK_ROWS * f_at, BACK_ROWS), back),
+            (forward_hbm, now_ref.at[0:3]),
+            (adjoint_hbm, now_ref.at[3:6]),
+            (forward_last_hbm, last_ref.at[0:3]),
+            (adjoint_last_hbm, last_ref.at[3:6]),
+            (mass_hbm, mass_ref),
+        ),
+    )
+    grid_ref[...] = jnp.zeros(grid_ref.shape, f32)
+    copies[0].wait()
+    copies[1].wait()
     for t in range(3):
         for n in range(NODES):
             for ea in range(2):
@@ -391,13 +515,23 @@
                     moduli_ref[pl.ds(ea * 8 * PART + t * NODES + n, 8, stride=PART), :]
                     * float(WEIGHTS[n])
                 )
-        moduli_s[t] = product(order_ref[...], sample_high[0], sample_low[0])
+        high, low = halves(order_ref[...])
+        for r in range(7):
+            at = r * LANES
+            block = sample[at : at + LANES, :]
+            rest = sample[7 * LANES + at : 8 * LANES + at, :]
+            moduli_s[t, :, at : at + LANES] = (
+                jnp.dot(high, block, preferred_element_type=f32)
+                + jnp.dot(low, block, preferred_element_type=f32)
+                + jnp.dot(high, rest, preferred_element_type=f32)
+            )
+    copies[2].wait()
 
     @pl.loop(0, NODES)
     def _(n):
         rows = pl.ds(pl.multiple_of(n * 16, 16), 16)
         for side in range(2):
-            e = [strain_ref[side, v, rows, :] for v in range(6)]
+            e = [strain_ref[side * 6 + v, rows, :] for v in range(6)]
             for v in range(6):
                 total = None
                 for w in range(6):
@@ -407,8 +541,6 @@
                     )
                     total = term if total is None else total + term
                 stress_ref[side, v, rows, :] = total
-
-    grid_ref[...] = jnp.zeros(grid_ref.shape, f32)
 
     @pl.loop(0, 2)
     def _(side):
@@ -434,203 +566,235 @@
                 for i in range(5):
                     for j in range(5):
                         at = pl.ds((i * 5 + j) * 16 + ea * 8, 8)
-                        add(c, 1, i, j, radius_ref[at, :] * stress(v_p, i, j))
-
+                        add(c, 1, i, j, strain_ref[12, at, :] * stress(v_p, i, j))
+
+    for copy in copies[3:]:
+        copy.wait()
+    mass = mass_ref[...]
     for c in range(6):
         joined = jnp.concatenate([grid_ref[k, c] for k in range(4)], axis=1)
-        force = product(joined, back_high[0], back_low[0])
-        edge_out[c] = force[NEXT:ROWS, :]
-        now_ref, last_ref, out_ref = (
-            (forward_ref, forward_last_ref, forward_out)
-            if c < 3
-            else (adjoint_ref, adjoint_last_ref, adjoint_out)
-        )
-        out_ref[c % 3] = (
-            2.0 * now_ref[c % 3] - last_ref[c % 3] - mass_ref[...] * force[0:132, :]
-        )
-
-
-def edge_kernel(forward_ref, adjoint_ref, edge_ref, mass_ref, forward_out, adjoint_out):
-    forward_out[...] = forward_ref[...] - mass_ref[...] * edge_ref[0:3]
-    adjoint_out[...] = adjoint_ref[...] - mass_ref[...] * edge_ref[3:6]
-
-
-def collect_kernel(terms_ref, out_ref):
+        force = product(joined, back[: 4 * LANES, :], back[4 * LANES :, :])
+        edge_ref[c] = force[NEXT:ROWS, :]
+        out_ref[c] = 2.0 * now_ref[c] - last_ref[c] - mass * force[0:132, :]
+    for copy in started(
+        out_sems,
+        (
+            (edge_ref, edge_hbm),
+            (out_ref.at[0:3], forward_out),
+            (out_ref.at[3:6], adjoint_out),
+        ),
+    ):
+        copy.wait()
+
+
+def finish_kernel(
+    forward_hbm,
+    adjoint_hbm,
+    edge_hbm,
+    mass_hbm,
+    terms_hbm,
+    forward_out,
+    adjoint_out,
+    kernel_hbm,
+    rows,
+    edge_ref,
+    mass_ref,
+    terms_ref,
+    kernel_ref,
+    sems,
+    out_sems,
+):
+    copies = started(
+        sems,
+        (
+            (forward_hbm.at[:, 0:24, :], rows.at[0:3]),
+            (adjoint_hbm.at[:, 0:24, :], rows.at[3:6]),
+            (edge_hbm, edge_ref),
+            (mass_hbm.at[0:24, :], mass_ref),
+            (terms_hbm, terms_ref),
+        ),
+    )
+    for copy in copies[:4]:
+        copy.wait()
+    mass = mass_ref[...]
+    for c in range(6):
+        rows[c] = rows[c] - mass * edge_ref[c]
+    copies[4].wait()
     total = terms_ref[0]
     for e in range(1, PEERS):
         total = total + terms_ref[e]
     for t in range(3):
         turned = jnp.transpose(total[t * NODES : t * NODES + NODES, :])
-        out_ref[119 * t : 119 * t + 119, :] = turned[0:119, :]
+        for r in range(7):
+            kernel_ref[7 * t + r, :, 0, :] = turned[17 * r : 17 * r + 17, :]
+    for copy in started(
+        out_sems,
+        (
+            (rows.at[0:3], forward_out.at[:, 0:24, :]),
+            (rows.at[3:6], adjoint_out.at[:, 0:24, :]),
+            (kernel_ref, kernel_hbm),
+        ),
+    ):
+        copy.wait()
 
 
 def shape(*dims):
     return jax.ShapeDtypeStruct(dims, f32)
 
 
-def whole(*dims):
-    return pl.BlockSpec(dims, lambda i, f: (0,) * len(dims))
-
-
-def picked(*dims):
-    return pl.BlockSpec((1, *dims), lambda i, f: (f[0],) + (0,) * len(dims))
-
-
-def kinded(*dims):
-    return pl.BlockSpec(
-        (1, *dims), lambda i, f: (jnp.minimum(f[0], 1),) + (0,) * len(dims)
+SMEM = pl.BlockSpec(memory_space=pltpu.SMEM)
+HBM = pl.BlockSpec(memory_space=pltpu.HBM)
+DMA = pltpu.SemaphoreType.DMA
+VMEM = pltpu.VMEM
+
+
+def call(kernel, name, us, ins, outs, scratch, aliases=None, limit=LIMIT):
+    return pl.pallas_call(
+        kernel,
+        in_specs=ins,
+        out_specs=(HBM,) * len(outs),
+        out_shape=outs,
+        scratch_shapes=scratch,
+        input_output_aliases=aliases or {},
+        compiler_params=pltpu.CompilerParams(vmem_limit_bytes=limit),
+        cost_estimate=pl.CostEstimate(
+            flops=int(us * 1e6), bytes_accessed=int(us * 3.0e6), transcendentals=0
+        ),
+        name=name,
     )
 
 
-def scalars():
-    return pl.BlockSpec(memory_space=pltpu.SMEM)
-
-
-def params(mib):
-    return pltpu.CompilerParams(vmem_limit_bytes=mib * 1024 * 1024)
-
-
-def cost(us):
-    return pl.CostEstimate(flops=int(us * 1e6), bytes_accessed=int(us * 3.0e6), transcendentals=0)
+def swaps(first):
+    route = []
+    for i in range(first, PEERS + first, 2):
+        route += [(i, (i + 1) % PEERS), ((i + 1) % PEERS, i)]
+    return route
 
 
 def body(forward_now, forward_last, adjoint_now, adjoint_last, moduli, inv_radius, inv_mass):
-    f_at = lax.axis_index(FOURIER).astype(jnp.int32).reshape(1)
     slices = lax.axis_size(MERIDIAN)
-    wave_high, wave_low = in_two(forward_tables())
-    back_high, back_low = in_two(inverse_tables())
-    sampling, projection = moduli_tables()
-    sample_high, sample_low = in_two(sampling)
-    project_high, project_low = in_two(projection)
-    weights = jnp.asarray(WEIGHTS, f32)
-
-    first_rows = jnp.concatenate([forward_now[:, :24], adjoint_now[:, :24]], axis=0)
-    next_rows = lax.ppermute(first_rows, MERIDIAN, [(s, s - 1) for s in range(1, slices)])
-
-    spread = pl.pallas_call(
-        spread_moduli_kernel,
-        out_shape=shape(PEERS, PART, LANES),
-        compiler_params=params(8),
-        cost_estimate=cost(2),
-        name="spread",
-    )(moduli.reshape(357, NODES))
-    gathered = lax.all_to_all(spread, FOURIER, 0, 0, tiled=True).reshape(PEERS * PART, LANES)
+    wave = np.stack(in_two(forward_tables()), axis=1)
+    tables = narrow_tables()
+    halo = (6, CHUNK, LANES)
+
+    now = jnp.concatenate([forward_now, adjoint_now], axis=0)
+    next_rows = lax.ppermute(now[:, :24], MERIDIAN, [(s, s - 1) for s in range(1, slices)])
 
     radius = jnp.broadcast_to(
         jnp.transpose(inv_radius.reshape(16, NODES)).reshape(400, 1), (400, LANES)
     )
-    mass = jnp.tile(inv_mass.reshape(132, 2), (1, 64))
-
-    x, top, low = pl.pallas_call(
+    pair = inv_mass.reshape(132, 2)
+    even = lax.broadcasted_iota(jnp.int32, (132, LANES), 1) % 2 == 0
+    mass = jnp.where(even, pair[:, 0:1], pair[:, 1:2])
+
+    spread = call(
+        spread_kernel,
+        "spread",
+        4,
+        [HBM],
+        (shape(PEERS, PART, LANES),),
+        [
+            VMEM((21, 17, 1, NODES), f32),
+            VMEM((PART, LANES), f32),
+            DMA((1,)),
+            DMA((PEERS,)),
+        ],
+        limit=62 * 1024 * 1024,
+    )(moduli)[0]
+    next_rows, spread, radius, mass = lax.optimization_barrier((next_rows, spread, radius, mass))
+    far, near, top = call(
         pack_kernel,
-        out_shape=(shape(6, ROWS, LANES), shape(6, CHUNK, LANES), shape(6, CHUNK, LANES)),
-        compiler_params=params(8),
-        cost_estimate=cost(2),
-        name="pack",
-    )(forward_now, adjoint_now, next_rows)
-    left = lax.ppermute(top, FOURIER, [(i, (i + 1) % PEERS) for i in range(PEERS)])
-    right = lax.ppermute(low, FOURIER, [(i, (i - 1) % PEERS) for i in range(PEERS)])
-
-    strain, terms = pl.pallas_call(
+        "pack",
+        2,
+        [HBM] * 2,
+        (shape(*halo), shape(*halo), shape(*halo)),
+        [VMEM((6, ROWS, LANES), f32), VMEM(halo, f32), VMEM(halo, f32), DMA((2,)), DMA((3,))],
+    )(now, next_rows)
+    far_in = lax.ppermute(far, FOURIER, swaps(1))
+    near_in = lax.ppermute(near, FOURIER, swaps(0))
+    spread, far_in, near_in = lax.optimization_barrier((spread, far_in, near_in))
+    gathered = lax.all_to_all(spread, FOURIER, 0, 0, tiled=True).reshape(PEERS * PART, LANES)
+
+    strain, terms = call(
         strain_kernel,
-        grid_spec=pltpu.PrefetchScalarGridSpec(
-            num_scalar_prefetch=1,
-            grid=(1,),
-            in_specs=[
-                whole(6, ROWS, LANES),
-                whole(6, CHUNK, LANES),
-                whole(6, CHUNK, LANES),
-                whole(6, CHUNK, LANES),
-                picked(2 * LANES, 4 * LANES),
-                picked(2 * LANES, 4 * LANES),
-                kinded(7 * LANES, LANES),
-                kinded(7 * LANES, LANES),
-                whole(400, LANES),
-                scalars(),
-            ],
-            out_specs=(whole(2, 6, 400, LANES), whole(PEERS * PART, LANES)),
-            scratch_shapes=[
-                pltpu.VMEM((6, ROWS, LANES), f32),
-                pltpu.VMEM((3, 3, 4, ROWS, LANES), f32),
-                pltpu.VMEM((3, 6, 400, LANES), f32),
-                pltpu.VMEM((400, 21 * LANES), bf16),
-                pltpu.VMEM((400, 21 * LANES), bf16),
-                pltpu.VMEM((400, LANES), f32),
-            ],
-        ),
-        out_shape=(shape(2, 6, 400, LANES), shape(PEERS * PART, LANES)),
-        compiler_params=params(40),
-        cost_estimate=cost(8),
-        name="strain",
+        "strain",
+        8,
+        [HBM] * 8,
+        (shape(13, 400, LANES), shape(PEERS * PART, LANES)),
+        [
+            VMEM((6, ROWS, LANES), f32),
+            VMEM((2, *halo), f32),
+            VMEM(halo, f32),
+            VMEM((2, 2 * LANES, 4 * LANES), bf16),
+            VMEM((KIND_ROWS, LANES), bf16),
+            VMEM((400, LANES), f32),
+            VMEM((12, 400, LANES), f32),
+            VMEM((6, ROWS, LANES), f32),
+            VMEM((3, 3, 4, ROWS, LANES), f32),
+            VMEM((6, 400, LANES), f32),
+            VMEM((400, 21 * LANES), bf16),
+            VMEM((400, 21 * LANES), bf16),
+            VMEM((400, LANES), f32),
+            VMEM((PEERS * PART, LANES), f32),
+            DMA((8,)),
+            DMA((3,)),
+        ],
+    )(now, next_rows, far_in, near_in, top, wave, tables, radius)
+    arrived = lax.all_to_all(terms.reshape(PEERS, PART, LANES), FOURIER, 0, 0, tiled=True)
+
+    forward_part, adjoint_part, edge = call(
+        stress_kernel,
+        "stress",
+        8,
+        [HBM] * 8,
+        (shape(3, 132, LANES), shape(3, 132, LANES), shape(6, 24, LANES)),
+        [
+            VMEM((PEERS * PART, LANES), f32),
+            VMEM((KIND_ROWS, LANES), bf16),
+            VMEM((13, 400, LANES), f32),
+            VMEM((BACK_ROWS, LANES), bf16),
+            VMEM((6, 132, LANES), f32),
+            VMEM((6, 132, LANES), f32),
+            VMEM((132, LANES), f32),
+            VMEM((6, 132, LANES), f32),
+            VMEM((6, 24, LANES), f32),
+            VMEM((400, LANES), f32),
+            VMEM((3, 400, 7 * LANES), f32),
+            VMEM((2, 6, 400, LANES), f32),
+            VMEM((NODES, 8, LANES), f32),
+            VMEM((4, 6, ROWS, LANES), f32),
+            DMA((9,)),
+            DMA((3,)),
+        ],
+        limit=62 * 1024 * 1024,
     )(
-        f_at, x, left, right, top, wave_high, wave_low, project_high, project_low, radius, weights
-    )
-    arrived = lax.all_to_all(
-        terms.reshape(PEERS, PART, LANES), FOURIER, 0, 0, tiled=True
-    )
-
-    field = whole(3, 132, LANES)
-    forward_part, adjoint_part, edge = pl.pallas_call(
-        stress_kernel,
-        grid_spec=pltpu.PrefetchScalarGridSpec(
-            num_scalar_prefetch=1,
-            grid=(1,),
-            in_specs=[
-                whole(2, 6, 400, LANES),
-                whole(PEERS * PART, LANES),
-                kinded(LANES, 7 * LANES),
-                kinded(LANES, 7 * LANES),
-                picked(4 * LANES, LANES),
-                picked(4 * LANES, LANES),
-                whole(400, LANES),
-                scalars(),
-                field,
-                field,
-                field,
-                field,
-                whole(132, LANES),
-            ],
-            out_specs=(field, field, whole(6, 24, LANES)),
-            scratch_shapes=[
-                pltpu.VMEM((400, LANES), f32),
-                pltpu.VMEM((3, 400, 7 * LANES), f32),
-                pltpu.VMEM((2, 6, 400, LANES), f32),
-                pltpu.VMEM((NODES, 8, LANES), f32),
-                pltpu.VMEM((4, 6, ROWS, LANES), f32),
-            ],
-        ),
-        out_shape=(shape(3, 132, LANES), shape(3, 132, LANES), shape(6, 24, LANES)),
-        compiler_params=params(40),
-        cost_estimate=cost(8),
-        name="stress",
-    )(
-        f_at, strain, gathered, sample_high, sample_low, back_high, back_low, radius, weights,
-        forward_now, forward_last, adjoint_now, adjoint_last, mass,
+        gathered,
+        tables,
+        strain,
+        forward_now,
+        adjoint_now,
+        forward_last,
+        adjoint_last,
+        mass,
     )
     carried = lax.ppermute(edge, MERIDIAN, [(s, s + 1) for s in range(slices - 1)])
-    first = pl.BlockSpec((3, 24, LANES), lambda i: (0, 0, 0))
-    forward_next, adjoint_next = pl.pallas_call(
-        edge_kernel,
-        grid=(1,),
-        in_specs=[
-            first,
-            first,
-            pl.BlockSpec((6, 24, LANES), lambda i: (0, 0, 0)),
-            pl.BlockSpec((24, LANES), lambda i: (0, 0)),
+    return call(
+        finish_kernel,
+        "finish",
+        2,
+        [HBM] * 5,
+        (shape(3, 132, LANES), shape(3, 132, LANES), shape(21, 17, 1, NODES)),
+        [
+            VMEM((6, 24, LANES), f32),
+            VMEM((6, 24, LANES), f32),
+            VMEM((24, LANES), f32),
+            VMEM((PEERS, PART, LANES), f32),
+            VMEM((21, 17, 1, NODES), f32),
+            DMA((5,)),
+            DMA((3,)),
         ],
-        out_specs=(first, first),
-        out_shape=(shape(3, 132, LANES), shape(3, 132, LANES)),
-        input_output_aliases={0: 0, 1: 1},
-        compiler_params=params(8),
-        name="edge",
-    )(forward_part, adjoint_part, carried, mass)
-    kernel = pl.pallas_call(
-        collect_kernel,
-        out_shape=shape(357, NODES),
-        compiler_params=params(8),
-        name="collect",
-    )(arrived)
-    return forward_next, adjoint_next, kernel.reshape(21, 17, 1, NODES)
+        {0: 0, 1: 1},
+    )(forward_part, adjoint_part, carried, mass, arrived)
 
 
 def solution(mesh):

time: 90.4 us -> 66.2 us (0.73)
  local copies, waits for them, and re-layouts: 26 us -> 3.95 us
  Pallas kernels: 15.6 us -> 21.6 us
  starting transfers between devices: 30.6 us -> 25.7 us
  waiting for transfers between devices: 14.8 us -> 12.8 us
    unnamed x48 -> x5, local copies, waits for them, and re-layouts: 21.2 us -> 0.96 us
    pallas_call x6 -> x5, Pallas kernels: 15.6 us -> 21.6 us  [the longest x1 8.67 us: body(): call(stress_kernel, 'stress', 8, [HBM] * 8, (shape(3, 132, LANES), shape(...]
    ppermute x3, waiting for transfers between devices: 8.35 us -> 3.56 us  [the longest x1 3.56 us: body(): far_in = lax.ppermute(far, FOURIER, swaps(1))]
    another operation x5 -> x0, local copies, waits for them, and re-layouts: 3.56 us -> none  [body(): mass = jnp.tile(inv_mass.reshape(132, 2), (1, 64))]
    ppermute x3, starting transfers between devices: 13.9 us -> 11 us  [the longest x1 4.76 us: body(): lax.ppermute(now[:, :24], MERIDIAN, [(s, s - 1) for s in range(1, slices)])]
    all_to_all x1, waiting for transfers between devices: 0.01 us -> 2.59 us  [body(): lax.all_to_all(spread, FOURIER, 0, 0, tiled=True)]
    unnamed x1 -> x0, other arithmetic: 1.49 us -> none
    all_to_all x1, starting transfers between devices: 7.45 us -> 6.43 us  [body(): lax.all_to_all(spread, FOURIER, 0, 0, tiled=True)]
  transfers between devices with their start and end apart: 6 -> 6, of which waited for: 4 -> 4; matrix products, arithmetic and copies ran while one was open for 4% -> 4% of each run, Pallas kernels for 16% -> 29%
where the time goes in v1:
time: 66.2 us; the launch traced here: 65.6 us
  starting transfers between devices  25.7 us (39%)
  Pallas kernels  21.6 us (33%)
  waiting for transfers between devices  12.8 us (19%)
  local copies, waits for them, and re-layouts  3.95 us (6%)
  between operations  0.77 us (1%)
  other arithmetic  0.74 us (1%)
    pallas_call x1, Pallas kernels, body(): call(stress_kernel, 'stress', 8, [HBM] * 8, (shape(3, 132, LANES), shape(...  8.67 us
    pallas_call x1, Pallas kernels, body(): call(strain_kernel, 'strain', 8, [HBM] * 8, (shape(13, 400, LANES), shape...  8.29 us
    all_to_all x1, starting transfers between devices, body(): lax.all_to_all(spread, FOURIER, 0, 0, tiled=True)  6.43 us
    all_to_all x1, starting transfers between devices, body(): lax.all_to_all(terms.reshape(PEERS, PART, LANES), FOURIER, 0, 0, tiled=True)  6.39 us
    ppermute x1, waiting for transfers between devices, body(): lax.ppermute(edge, MERIDIAN, [(s, s + 1) for s in range(slices - 1)])  6.33 us
    ppermute x1, starting transfers between devices, body(): lax.ppermute(now[:, :24], MERIDIAN, [(s, s - 1) for s in range(1, slices)])  4.76 us
    ppermute x1, starting transfers between devices, body(): far_in = lax.ppermute(far, FOURIER, swaps(1))  4.32 us
    ppermute x1, waiting for transfers between devices, body(): far_in = lax.ppermute(far, FOURIER, swaps(1))  3.56 us
  transfers between devices with their start and end apart: 6, of which 4 were waited for; matrix products, arithmetic and copies ran while one was open for 4% of the time, Pallas kernels for 29%

profile of v1, /device:TPU:388, one launch (start us, length us, event | category | flops | bytes accessed | tf_op | source)
XLA Modules:
  0.0 65.6 jit_solution(16780902877628803104)
XLA Ops:
  0.6 0.9 %constant_dynamic-update-slice_fusion.1 = f32[6,132,128]{2,1,0:T(8,128)S(1)} fusion(f32[3,132,128]{2,1,0:T(8,128)} %forward_hbm.1), kind=kLoop, calls=%fused_computation.5 | loop fusion | bytes 411648
  1.6 0.9 %constant_dynamic-update-slice_fusion.now_hbm = f32[6,132,128]{2,1,0:T(8,128)S(1)} fusion(f32[6,132,128]{2,1,0:T(8,128)S(1)} %constant_dynamic-update-slice_fusion.1, f32[3,132,128]{2,1,0:T(8,128)} %adjoint_hbm.1), kind=kLoop, calls=%fused_computation.4 | loop fusion | bytes 411648 | tf_op jit(solution)/shard_map/concatenate | solution.py:680
  2.5 4.8 %collective-permute-start = (f32[6,24,128]{2,1,0:T(8,128)S(1)}, f32[6,24,128]{2,1,0:T(8,128)S(1)}, u32[]{:S(2)}, u32[]{:S(2)}) collective-permute-start(f32[6,24,128]{2,1,0:T(8,128)S(1)} %slice.12), channel_id=1, source_target_pairs={{1,0},{2,1},{3,2},{4,3},{5,4},{6,5},{7,6},{8,7},{9,8},{10,9},{11,1... | collective-permute-start | bytes 221192 | tf_op jit(solution)/shard_map/ppermute | solution.py:681
  7.3 0.8 %reshape.21 = f32[132,2]{1,0:T(8,128)S(1)} reshape(f32[264]{0:T(512)} %param.15) | data formatting | bytes 2112 | tf_op jit(solution)/shard_map/reshape | solution.py:686
  8.2 0.2 slice_reduce_fusion.1
  8.3 0.7 %fusion.mass_hbm = f32[132,128]{1,0:T(8,128)} fusion(f32[132]{0:T(256)S(1)} %get-tuple-element.34, f32[132]{0:T(256)S(1)} %get-tuple-element.33, s32[128]{0:T(128)S(1)} %get-tuple-element.35, s32[128]{0:T(128)S(1)} %get-tuple-element.36, pred[128]{0:T(512)(128)(4,1)S(1)} %compare_and_fusion), kind=kLoop, calls=%fused_computation.3 | loop fusion | flops 50688 | bytes 69792 | tf_op jit(solution)/shard_map/jit(_where)/select_n | solution.py:688
  9.1 0.8 %reshape.20 = f32[16,25]{1,0:T(8,128)S(1)} reshape(f32[400]{0:T(512)} %param.14) | data formatting | bytes 3200 | tf_op jit(solution)/shard_map/reshape | solution.py:684
  9.8 0.1 copy.14
  9.9 0.1 broadcast_in_dim.27
  10.0 2.1 %spread.1 = f32[16,80,128]{2,1,0:T(8,128)} custom-call(f32[21,17,1,25]{3,2,1,0:T(1,128)} %moduli_hbm.1), custom_call_target="tpu_custom_call" | custom-call | flops 4000000 | bytes 12000000 | tf_op jit(solution)/shard_map/spread/pallas_call | solution.py:690
  12.1 0.0 collective-permute-done.next_hbm
  12.1 0.1 broadcast_in_dim.28.radius_hbm
  12.2 0.8 %pack.1 = (f32[6,40,128]{2,1,0:T(8,128)S(1)}, f32[6,40,128]{2,1,0:T(8,128)S(1)}, f32[6,40,128]{2,1,0:T(8,128)S(1)}) custom-call(f32[6,132,128]{2,1,0:T(8,128)S(1)} %constant_dynamic-update-slice_fusion.now_hbm, f32[6,24,128]{2,1,0:T(8,128)S(1)} %collective-permute-done.next_hbm), custom_call_target="tpu_custom_call" | custom-call | flops 2000000 | bytes 6000000 | tf_op jit(solution)/shard_map/pack/pallas_call | solution.py:705
  13.1 4.3 %collective-permute-start.1 = (f32[6,40,128]{2,1,0:T(8,128)S(1)}, f32[6,40,128]{2,1,0:T(8,128)S(1)}, u32[]{:S(2)}, u32[]{:S(2)}) collective-permute-start(f32[6,40,128]{2,1,0:T(8,128)S(1)} %get-tuple-element.20), channel_id=1, source_target_pairs={{32,64},{64,32},{96,128},{128,96},{160,192},{192,160},{224,256},{2... | collective-permute-start | bytes 368648 | tf_op jit(solution)/shard_map/ppermute | solution.py:713
  17.4 1.9 %collective-permute-start.2 = (f32[6,40,128]{2,1,0:T(8,128)S(1)}, f32[6,40,128]{2,1,0:T(8,128)S(1)}, u32[]{:S(2)}, u32[]{:S(2)}) collective-permute-start(f32[6,40,128]{2,1,0:T(8,128)S(1)} %get-tuple-element.21), channel_id=1, source_target_pairs={{0,32},{32,0},{64,96},{96,64},{128,160},{160,128},{192,224},{224,1... | collective-permute-start | bytes 368648 | tf_op jit(solution)/shard_map/ppermute | solution.py:714
  19.3 3.6 %collective-permute-done.1.far_hbm = f32[6,40,128]{2,1,0:T(8,128)S(1)} collective-permute-done((f32[6,40,128]{2,1,0:T(8,128)S(1)}, f32[6,40,128]{2,1,0:T(8,128)S(1)}, u32[]{:S(2)}, u32[]{:S(2)}) %collective-permute-start.1) | collective-permute-done | bytes 122912 | tf_op jit(solution)/shard_map/ppermute | solution.py:713
  22.9 0.0 collective-permute-done.2.near_hbm
  22.9 6.4 %all-to-all-start = ((f32[16,80,128]{2,1,0:T(8,128)}), f32[16,80,128]{2,1,0:T(8,128)S(1)}, u32[]{:S(2)}, u32[]{:S(2)}) async-start(f32[16,80,128]{2,1,0:T(8,128)} %spread.1), calls=%async_computation | async-start | bytes 1310720 | tf_op jit(solution)/shard_map/all_to_all | solution.py:716
  29.3 8.3 %strain.1 = (f32[13,400,128]{2,1,0:T(8,128)}, f32[1280,128]{1,0:T(8,128)}) custom-call(f32[6,132,128]{2,1,0:T(8,128)S(1)} %constant_dynamic-update-slice_fusion.now_hbm, f32[6,24,128]{2,1,0:T(8,128)S(1)} %collective-permute-done.next_hbm, f32[6,40,128]{2,1,0:T(8,128)S(1)} %collective-permute-done.1.far_hbm, ...), custom_call_target="tpu_custom_call" | custom-call | flops 8000000 | bytes 24000000 | tf_op jit(solution)/shard_map/strain/pallas_call | solution.py:718
  37.6 0.0 copy-start
  37.6 2.6 %all-to-all-done = f32[16,80,128]{2,1,0:T(8,128)S(1)} async-done(((f32[16,80,128]{2,1,0:T(8,128)}), f32[16,80,128]{2,1,0:T(8,128)S(1)}, u32[]{:S(2)}, u32[]{:S(2)}) %all-to-all-start) | async-done | bytes 655392 | tf_op jit(solution)/shard_map/all_to_all | solution.py:716
  40.2 0.0 copy-start.1
  40.2 6.4 %all-to-all-start.1 = ((f32[16,80,128]{2,1,0:T(8,128)}), f32[16,80,128]{2,1,0:T(8,128)S(1)}, u32[]{:S(2)}, u32[]{:S(2)}) async-start(f32[16,80,128]{2,1,0:T(8,128)} %bitcast.2), calls=%async_computation.1 | async-start | bytes 1310720 | tf_op jit(solution)/shard_map/all_to_all | solution.py:743
  46.6 0.0 copy-done.1
  46.6 8.7 %stress.1 = (f32[3,132,128]{2,1,0:T(8,128)}, f32[3,132,128]{2,1,0:T(8,128)}, f32[6,24,128]{2,1,0:T(8,128)}) custom-call(f32[1280,128]{1,0:T(8,128)} %bitcast.3, bf16[23552,128]{1,0:T(8,128)(2,1)} %constant.22.clone.table_hbm, f32[13,400,128]{2,1,0:T(8,128)} %get-tuple-element.27.strain_hbm, f32[3,132,128]{2,1,0:T(8,128)} %forward_hbm.1, ...), custom_call_target="tpu_custom_call" | custom-call | flops 8000000 | bytes 24000000 | tf_op jit(solution)/shard_map/stress/pallas_call | solution.py:745
  55.3 1.9 %collective-permute-start.3 = (f32[6,24,128]{2,1,0:T(8,128)}, f32[6,24,128]{2,1,0:T(8,128)S(1)}, u32[]{:S(2)}, u32[]{:S(2)}) collective-permute-start(f32[6,24,128]{2,1,0:T(8,128)} %get-tuple-element.31), channel_id=1, source_target_pairs={{0,1},{1,2},{2,3},{3,4},{4,5},{5,6},{6,7},{7,8},{8,9},{9,10},{10,1... | collective-permute-start | bytes 221192 | tf_op jit(solution)/shard_map/ppermute | solution.py:780
  57.2 0.3 all-to-all-done.1.terms_hbm
  57.5 6.3 %collective-permute-done.3.edge_hbm = f32[6,24,128]{2,1,0:T(8,128)S(1)} collective-permute-done((f32[6,24,128]{2,1,0:T(8,128)}, f32[6,24,128]{2,1,0:T(8,128)S(1)}, u32[]{:S(2)}, u32[]{:S(2)}) %collective-permute-start.3) | collective-permute-done | bytes 73760 | tf_op jit(solution)/shard_map/ppermute | solution.py:780
  63.9 0.0 copy-done
  63.9 1.7 %finish.1 = (f32[3,132,128]{2,1,0:T(8,128)}, f32[3,132,128]{2,1,0:T(8,128)}, f32[21,17,1,25]{3,2,1,0:T(1,128)}) custom-call(f32[3,132,128]{2,1,0:T(8,128)} %get-tuple-element.29.forward_hbm, f32[3,132,128]{2,1,0:T(8,128)} %get-tuple-element.30.adjoint_hbm, ...), custom_call_target="tpu_custom_call", output_to_operand_aliasing={{0}: (0, {}), {1}: (1, {})} | custom-call | flops 2000000 | bytes 6000000 | tf_op jit(solution)/shard_map/finish/pallas_call | solution.py:781
  (3 shorter events, 0.0 us)
Async XLA Ops:
  2.5 9.5 %collective-permute-start = (f32[6,24,128]{2,1,0:T(8,128)S(1)}, f32[6,24,128]{2,1,0:T(8,128)S(1)}, u32[]{:S(2)}, u32[]{:S(2)}) collective-permute-start(f32[6,24,128]{2,1,0:T(8,128)S(1)} %slice.12), channel_id=1, source_target_pairs={{1,0},{2,1},{3,2},{4,3},{5,4},{6,5},{7,6},{8,7},{9,8},{10,9},{11,1... | collective-permute-start | bytes 221192 | tf_op jit(solution)/shard_map/ppermute | solution.py:681
  13.1 9.8 %collective-permute-start.1 = (f32[6,40,128]{2,1,0:T(8,128)S(1)}, f32[6,40,128]{2,1,0:T(8,128)S(1)}, u32[]{:S(2)}, u32[]{:S(2)}) collective-permute-start(f32[6,40,128]{2,1,0:T(8,128)S(1)} %get-tuple-element.20), channel_id=1, source_target_pairs={{32,64},{64,32},{96,128},{128,96},{160,192},{192,160},{224,256},{2... | collective-permute-start | bytes 368648 | tf_op jit(solution)/shard_map/ppermute | solution.py:713
  17.4 5.5 %collective-permute-start.2 = (f32[6,40,128]{2,1,0:T(8,128)S(1)}, f32[6,40,128]{2,1,0:T(8,128)S(1)}, u32[]{:S(2)}, u32[]{:S(2)}) collective-permute-start(f32[6,40,128]{2,1,0:T(8,128)S(1)} %get-tuple-element.21), channel_id=1, source_target_pairs={{0,32},{32,0},{64,96},{96,64},{128,160},{160,128},{192,224},{224,1... | collective-permute-start | bytes 368648 | tf_op jit(solution)/shard_map/ppermute | solution.py:714
  22.9 17.3 %all-to-all-start = ((f32[16,80,128]{2,1,0:T(8,128)}), f32[16,80,128]{2,1,0:T(8,128)S(1)}, u32[]{:S(2)}, u32[]{:S(2)}) async-start(f32[16,80,128]{2,1,0:T(8,128)} %spread.1), calls=%async_computation | async-start | bytes 1310720 | tf_op jit(solution)/shard_map/all_to_all | solution.py:716
  37.6 26.2 %copy-start = (f32[132,128]{1,0:T(8,128)S(1)}, f32[132,128]{1,0:T(8,128)}, u32[]{:S(2)}) copy-start(f32[132,128]{1,0:T(8,128)} %fusion.mass_hbm) | copy-start | bytes 202756
  40.2 6.4 %copy-start.1 = (f32[16,80,128]{2,1,0:T(8,128)}, f32[16,80,128]{2,1,0:T(8,128)S(1)}, u32[]{:S(2)}) copy-start(f32[16,80,128]{2,1,0:T(8,128)S(1)} %all-to-all-done) | copy-start | bytes 1966084
  40.2 17.3 %all-to-all-start.1 = ((f32[16,80,128]{2,1,0:T(8,128)}), f32[16,80,128]{2,1,0:T(8,128)S(1)}, u32[]{:S(2)}, u32[]{:S(2)}) async-start(f32[16,80,128]{2,1,0:T(8,128)} %bitcast.2), calls=%async_computation.1 | async-start | bytes 1310720 | tf_op jit(solution)/shard_map/all_to_all | solution.py:743
  55.3 8.6 %collective-permute-start.3 = (f32[6,24,128]{2,1,0:T(8,128)}, f32[6,24,128]{2,1,0:T(8,128)S(1)}, u32[]{:S(2)}, u32[]{:S(2)}) collective-permute-start(f32[6,24,128]{2,1,0:T(8,128)} %get-tuple-element.31), channel_id=1, source_target_pairs={{0,1},{1,2},{2,3},{3,4},{4,5},{5,6},{6,7},{7,8},{8,9},{9,10},{10,1... | collective-permute-start | bytes 221192 | tf_op jit(solution)/shard_map/ppermute | solution.py:780

commit v2 on v1

--- a/solution.py
+++ b/solution.py
@@ -161,15 +161,12 @@
 BACK_ROWS = 2 * 4 * LANES
 KIND_ROWS = 2 * 7 * LANES
 PROJECT_AT = PEERS * BACK_ROWS
-SAMPLE_AT = PROJECT_AT + 2 * KIND_ROWS
-
-
-def narrow_tables():
-    sampling, projection = moduli_tables()
-    blocks = np.stack(np.split(sampling, 7, axis=2), axis=1)
+
+
+def narrow_tables(projection):
     parts = [
         np.stack(in_two(table), axis=1).reshape(-1, LANES)
-        for table in (inverse_tables(), projection, blocks)
+        for table in (inverse_tables(), projection)
     ]
     return np.concatenate(parts)
 
@@ -218,12 +215,17 @@
     return high, (x - high.astype(f32)).astype(bf16)
 
 
-def product(x, high, low):
-    x_high, x_low = halves(x)
+def threes(x):
+    high, low = halves(x)
+    return jnp.concatenate([high, low, high], axis=1)
+
+
+def beside(high, low, table):
+    both = jnp.dot(high, table, preferred_element_type=f32)
     return (
-        jnp.dot(x_high, high, preferred_element_type=f32)
-        + jnp.dot(x_low, high, preferred_element_type=f32)
-        + jnp.dot(x_high, low, preferred_element_type=f32)
+        both[:, :LANES]
+        + both[:, LANES:]
+        + jnp.dot(low, table[:, :LANES], preferred_element_type=f32)
     )
 
 
@@ -259,12 +261,23 @@
 
 
 def pack_kernel(
-    now_hbm, next_hbm, far_hbm, near_hbm, top_hbm, x_ref, top_ref, low_ref, sems, out_sems
+    forward_hbm,
+    adjoint_hbm,
+    next_hbm,
+    far_hbm,
+    near_hbm,
+    top_hbm,
+    x_ref,
+    top_ref,
+    low_ref,
+    sems,
+    out_sems,
 ):
     copies = started(
         sems,
         (
-            (now_hbm, x_ref.at[:, 0:132, :]),
+            (forward_hbm, x_ref.at[0:3, 0:132, :]),
+            (adjoint_hbm, x_ref.at[3:6, 0:132, :]),
             (next_hbm, x_ref.at[:, NEXT:ROWS, :]),
         ),
     )
@@ -307,8 +320,45 @@
     top_copy.wait()
 
 
+def strains(sample_ref, which, radius_ref, out_ref, out_at):
+    for ea in range(2):
+
+        def node(c, turned, i, j):
+            row, parity = point_rows(ea, i, j)
+            return sample_ref[which, c, 2 * turned + parity, pl.ds(row, 8, stride=2), :]
+
+        def place(i, j):
+            return pl.ds((i * 5 + j) * 16 + ea * 8, 8)
+
+        def store(v, i, j, value, add):
+            at = (out_at + v, place(i, j), slice(None))
+            if add:
+                value = value + out_ref[at]
+            out_ref[at] = value
+
+        for c, v_a, v_b, v_p, add_a, add_b in (
+            (0, 0, 5, 4, False, False),
+            (1, 5, 1, 3, True, False),
+            (2, 4, 3, 2, True, True),
+        ):
+            for i in range(5):
+                for j in range(5):
+                    store(
+                        v_p, i, j, radius_ref[place(i, j), :] * node(c, 1, i, j), False
+                    )
+            for j in range(5):
+                line = apply_line(DERIVE, [node(c, 0, i, j) for i in range(5)])
+                for i in range(5):
+                    store(v_a, i, j, line[i], add_a)
+            for i in range(5):
+                line = apply_line(DERIVE, [node(c, 0, i, j) for j in range(5)])
+                for j in range(5):
+                    store(v_b, i, j, line[j], add_b)
+
+
 def strain_kernel(
-    now_hbm,
+    forward_hbm,
+    adjoint_hbm,
     next_hbm,
     far_hbm,
     near_hbm,
@@ -316,6 +366,7 @@
     wave_hbm,
     table_hbm,
     radius_hbm,
+    sample_hbm,
     strain_hbm,
     terms_hbm,
     x_ref,
@@ -342,14 +393,25 @@
             (far_hbm, beside_ref.at[lax.rem(f_at, 2)]),
             (near_hbm, beside_ref.at[1 - lax.rem(f_at, 2)]),
             (top_hbm, top_ref),
-            (wave_hbm.at[f_at], wave),
-            (now_hbm, x_ref.at[:, 0:132, :]),
+            (forward_hbm, x_ref.at[0:3, 0:132, :]),
+            (adjoint_hbm, x_ref.at[3:6, 0:132, :]),
             (next_hbm, x_ref.at[:, NEXT:ROWS, :]),
             (radius_hbm, radius_ref),
+        )
+        + tuple(
+            (wave_hbm.at[f_at, part], wave.at[k * LANES : (k + 1) * LANES, :])
+            for k, part in enumerate((0, 0, 2, 1, 1, 3))
+        )
+        + tuple(
             (
-                table_rows(table_hbm, PROJECT_AT + KIND_ROWS * jnp.minimum(f_at, 1), KIND_ROWS),
-                project,
-            ),
+                table_rows(
+                    table_hbm,
+                    PROJECT_AT + KIND_ROWS * jnp.minimum(f_at, 1) + 7 * LANES * k,
+                    7 * LANES,
+                ),
+                project.at[:, k * LANES : (k + 1) * LANES],
+            )
+            for k in range(2)
         ),
     )
     x_ref[:, 132:NEXT, :] = jnp.zeros((6, NEXT - 132, LANES), f32)
@@ -364,66 +426,31 @@
             d = top if g == 2 else pltpu.roll(top, (64 - 32 * g) % LANES, 1)
             rows = jnp.where(group == 0, a, jnp.where(group == 1, b, d))
             halo_ref[c, CHUNK * g : CHUNK * g + CHUNK, :] = jnp.where(group == 3, 0.0, rows)
-    for copy in copies[3:7]:
+    for copy in copies[3:13]:
         copy.wait()
-    radius_copy = pltpu.make_async_copy(radius_ref, strain_hbm.at[12], out_sems.at[2])
+    radius_copy = pltpu.make_async_copy(radius_ref, strain_hbm.at[6], out_sems.at[2])
     radius_copy.start()
     for c in range(6):
-        own = product(x_ref[c], wave[0, :LANES, :], wave[1, :LANES, :])
-        beside = product(halo_ref[c], wave[0, LANES:, :], wave[1, LANES:, :])
-        both = own + beside
+        own = jnp.dot(threes(x_ref[c]), wave[: 3 * LANES, :], preferred_element_type=f32)
+        both = own + jnp.dot(
+            threes(halo_ref[c]), wave[3 * LANES :, :], preferred_element_type=f32
+        )
         for k in range(4):
             sample_ref[c // 3, c % 3, k] = both[:, k * LANES : (k + 1) * LANES]
             if c < 3:
                 sample_ref[2, c, k] = own[:, k * LANES : (k + 1) * LANES]
 
-    def strains(which, out_ref, out_at):
-        for ea in range(2):
-
-            def node(c, turned, i, j):
-                row, parity = point_rows(ea, i, j)
-                return sample_ref[which, c, 2 * turned + parity, pl.ds(row, 8, stride=2), :]
-
-            def place(i, j):
-                return pl.ds((i * 5 + j) * 16 + ea * 8, 8)
-
-            def store(v, i, j, value, add):
-                at = (out_at + v, place(i, j), slice(None))
-                if add:
-                    value = value + out_ref[at]
-                out_ref[at] = value
-
-            for c, v_a, v_b, v_p, add_a, add_b in (
-                (0, 0, 5, 4, False, False),
-                (1, 5, 1, 3, True, False),
-                (2, 4, 3, 2, True, True),
-            ):
-                for i in range(5):
-                    for j in range(5):
-                        store(
-                            v_p, i, j, radius_ref[place(i, j), :] * node(c, 1, i, j), False
-                        )
-                for j in range(5):
-                    line = apply_line(DERIVE, [node(c, 0, i, j) for i in range(5)])
-                    for i in range(5):
-                        store(v_a, i, j, line[i], add_a)
-                for i in range(5):
-                    line = apply_line(DERIVE, [node(c, 0, i, j) for j in range(5)])
-                    for j in range(5):
-                        store(v_b, i, j, line[j], add_b)
-
-    @pl.loop(0, 2)
-    def _(which):
-        strains(which, strain_ref, which * 6)
-
-    strain_copy = pltpu.make_async_copy(strain_ref, strain_hbm.at[0:12], out_sems.at[0])
+    sample_copy = pltpu.make_async_copy(sample_ref.at[0], sample_hbm, out_sems.at[3])
+    sample_copy.start()
+    strains(sample_ref, 1, radius_ref, strain_ref, 0)
+    strain_copy = pltpu.make_async_copy(strain_ref, strain_hbm.at[0:6], out_sems.at[0])
     strain_copy.start()
-    strains(2, central_ref, 0)
+    strains(sample_ref, 2, radius_ref, central_ref, 0)
 
     @pl.loop(0, NODES)
     def _(n):
         rows = pl.ds(pl.multiple_of(n * 16, 16), 16)
-        a = [strain_ref[6 + v, rows, :] for v in range(6)]
+        a = [strain_ref[v, rows, :] for v in range(6)]
         f = [central_ref[v, rows, :] for v in range(6)]
         for v in range(6):
             for w in range(v, 6):
@@ -435,15 +462,12 @@
                 high_ref[rows, r * LANES : (r + 1) * LANES] = high
                 low_ref[rows, r * LANES : (r + 1) * LANES] = low
 
-    copies[7].wait()
+    copies[13].wait()
+    copies[14].wait()
     for t in range(3):
         cut = slice(t * 7 * LANES, (t + 1) * 7 * LANES)
         high, low = high_ref[:, cut], low_ref[:, cut]
-        sum_ref[...] = (
-            jnp.dot(high, project[: 7 * LANES, :], preferred_element_type=f32)
-            + jnp.dot(low, project[: 7 * LANES, :], preferred_element_type=f32)
-            + jnp.dot(high, project[7 * LANES :, :], preferred_element_type=f32)
-        )
+        sum_ref[...] = beside(high, low, project[...])
         for n in range(NODES):
             for ea in range(2):
                 terms_ref[pl.ds(ea * 8 * PART + t * NODES + n, 8, stride=PART), :] = sum_ref[
@@ -453,6 +477,7 @@
         terms_ref[e * PART + 75 : e * PART + PART, :] = jnp.zeros((PART - 75, LANES), f32)
     terms_copy = pltpu.make_async_copy(terms_ref, terms_hbm, out_sems.at[1])
     terms_copy.start()
+    sample_copy.wait()
     strain_copy.wait()
     radius_copy.wait()
     terms_copy.wait()
@@ -460,7 +485,9 @@
 
 def stress_kernel(
     moduli_hbm,
+    sample_hbm,
     table_hbm,
+    forward_samples_hbm,
     strain_hbm,
     forward_hbm,
     adjoint_hbm,
@@ -472,6 +499,7 @@
     edge_hbm,
     moduli_ref,
     sample,
+    forward_samples,
     strain_ref,
     back,
     now_ref,
@@ -488,16 +516,24 @@
     out_sems,
 ):
     f_at = lax.axis_index(FOURIER)
+    kind = jnp.minimum(f_at, 1)
     copies = started(
         sems,
         (
             (moduli_hbm, moduli_ref),
+            (sample_hbm.at[kind, 0], sample.at[0:LANES, :]),
+            (sample_hbm.at[kind, 0], sample.at[LANES : 2 * LANES, :]),
+            (sample_hbm.at[kind, 1], sample.at[2 * LANES :, :]),
+            (forward_samples_hbm, forward_samples.at[0]),
+            (strain_hbm, strain_ref.at[6:13]),
             (
-                table_rows(table_hbm, SAMPLE_AT + KIND_ROWS * jnp.minimum(f_at, 1), KIND_ROWS),
-                sample,
+                table_rows(table_hbm, BACK_ROWS * f_at, 4 * LANES),
+                back.at[:, 0:LANES],
             ),
-            (strain_hbm, strain_ref),
-            (table_rows(table_hbm, BACK_ROWS * f_at, BACK_ROWS), back),
+            (
+                table_rows(table_hbm, BACK_ROWS * f_at + 4 * LANES, 4 * LANES),
+                back.at[:, LANES : 2 * LANES],
+            ),
             (forward_hbm, now_ref.at[0:3]),
             (adjoint_hbm, now_ref.at[3:6]),
             (forward_last_hbm, last_ref.at[0:3]),
@@ -506,8 +542,8 @@
         ),
     )
     grid_ref[...] = jnp.zeros(grid_ref.shape, f32)
-    copies[0].wait()
-    copies[1].wait()
+    for copy in copies[:4]:
+        copy.wait()
     for t in range(3):
         for n in range(NODES):
             for ea in range(2):
@@ -515,17 +551,12 @@
                     moduli_ref[pl.ds(ea * 8 * PART + t * NODES + n, 8, stride=PART), :]
                     * float(WEIGHTS[n])
                 )
-        high, low = halves(order_ref[...])
-        for r in range(7):
-            at = r * LANES
-            block = sample[at : at + LANES, :]
-            rest = sample[7 * LANES + at : 8 * LANES + at, :]
-            moduli_s[t, :, at : at + LANES] = (
-                jnp.dot(high, block, preferred_element_type=f32)
-                + jnp.dot(low, block, preferred_element_type=f32)
-                + jnp.dot(high, rest, preferred_element_type=f32)
-            )
-    copies[2].wait()
+        moduli_s[t] = jnp.dot(
+            threes(order_ref[...]), sample[...], preferred_element_type=f32
+        )
+    copies[4].wait()
+    copies[5].wait()
+    strains(forward_samples, 0, strain_ref.at[12], strain_ref, 0)
 
     @pl.loop(0, NODES)
     def _(n):
@@ -568,12 +599,12 @@
                         at = pl.ds((i * 5 + j) * 16 + ea * 8, 8)
                         add(c, 1, i, j, strain_ref[12, at, :] * stress(v_p, i, j))
 
-    for copy in copies[3:]:
+    for copy in copies[6:]:
         copy.wait()
     mass = mass_ref[...]
     for c in range(6):
         joined = jnp.concatenate([grid_ref[k, c] for k in range(4)], axis=1)
-        force = product(joined, back[: 4 * LANES, :], back[4 * LANES :, :])
+        force = beside(*halves(joined), back[...])
         edge_ref[c] = force[NEXT:ROWS, :]
         out_ref[c] = 2.0 * now_ref[c] - last_ref[c] - mass * force[0:132, :]
     for copy in started(
@@ -673,20 +704,14 @@
 
 def body(forward_now, forward_last, adjoint_now, adjoint_last, moduli, inv_radius, inv_mass):
     slices = lax.axis_size(MERIDIAN)
-    wave = np.stack(in_two(forward_tables()), axis=1)
-    tables = narrow_tables()
+    wave = np.stack(in_two(forward_tables()), axis=1).reshape(PEERS, 4, LANES, 4 * LANES)
+    sampling, projection = moduli_tables()
+    sample = np.stack(in_two(sampling), axis=1)
+    tables = narrow_tables(projection)
     halo = (6, CHUNK, LANES)
 
-    now = jnp.concatenate([forward_now, adjoint_now], axis=0)
-    next_rows = lax.ppermute(now[:, :24], MERIDIAN, [(s, s - 1) for s in range(1, slices)])
-
-    radius = jnp.broadcast_to(
-        jnp.transpose(inv_radius.reshape(16, NODES)).reshape(400, 1), (400, LANES)
-    )
-    pair = inv_mass.reshape(132, 2)
-    even = lax.broadcasted_iota(jnp.int32, (132, LANES), 1) % 2 == 0
-    mass = jnp.where(even, pair[:, 0:1], pair[:, 1:2])
-
+    first_rows = jnp.concatenate([forward_now[:, :24], adjoint_now[:, :24]], axis=0)
+    moduli, first_rows = lax.optimization_barrier((moduli, first_rows))
     spread = call(
         spread_kernel,
         "spread",
@@ -701,34 +726,47 @@
         ],
         limit=62 * 1024 * 1024,
     )(moduli)[0]
-    next_rows, spread, radius, mass = lax.optimization_barrier((next_rows, spread, radius, mass))
+    gathered = lax.all_to_all(spread, FOURIER, 0, 0, tiled=True).reshape(PEERS * PART, LANES)
+    next_rows = lax.ppermute(first_rows, MERIDIAN, [(s, s - 1) for s in range(1, slices)])
+
+    pair = inv_mass.reshape(132, 2)
+    even = lax.broadcasted_iota(jnp.int32, (132, LANES), 1) % 2 == 0
+    mass = jnp.where(even, pair[:, 0:1], pair[:, 1:2])
+    next_rows, mass = lax.optimization_barrier((next_rows, mass))
     far, near, top = call(
         pack_kernel,
         "pack",
         2,
-        [HBM] * 2,
+        [HBM] * 3,
         (shape(*halo), shape(*halo), shape(*halo)),
-        [VMEM((6, ROWS, LANES), f32), VMEM(halo, f32), VMEM(halo, f32), DMA((2,)), DMA((3,))],
-    )(now, next_rows)
+        [VMEM((6, ROWS, LANES), f32), VMEM(halo, f32), VMEM(halo, f32), DMA((3,)), DMA((3,))],
+        limit=62 * 1024 * 1024,
+    )(forward_now, adjoint_now, next_rows)
     far_in = lax.ppermute(far, FOURIER, swaps(1))
     near_in = lax.ppermute(near, FOURIER, swaps(0))
-    spread, far_in, near_in = lax.optimization_barrier((spread, far_in, near_in))
-    gathered = lax.all_to_all(spread, FOURIER, 0, 0, tiled=True).reshape(PEERS * PART, LANES)
-
-    strain, terms = call(
+    inv_radius, top = lax.optimization_barrier((inv_radius, top))
+    radius = jnp.broadcast_to(
+        jnp.transpose(inv_radius.reshape(16, NODES)).reshape(400, 1), (400, LANES)
+    )
+    radius, mass = lax.optimization_barrier((radius, mass))
+    samples, strain, terms = call(
         strain_kernel,
         "strain",
         8,
-        [HBM] * 8,
-        (shape(13, 400, LANES), shape(PEERS * PART, LANES)),
+        [HBM] * 9,
+        (
+            shape(3, 4, ROWS, LANES),
+            shape(7, 400, LANES),
+            shape(PEERS * PART, LANES),
+        ),
         [
             VMEM((6, ROWS, LANES), f32),
             VMEM((2, *halo), f32),
             VMEM(halo, f32),
-            VMEM((2, 2 * LANES, 4 * LANES), bf16),
-            VMEM((KIND_ROWS, LANES), bf16),
+            VMEM((6 * LANES, 4 * LANES), bf16),
+            VMEM((7 * LANES, 2 * LANES), bf16),
             VMEM((400, LANES), f32),
-            VMEM((12, 400, LANES), f32),
+            VMEM((6, 400, LANES), f32),
             VMEM((6, ROWS, LANES), f32),
             VMEM((3, 3, 4, ROWS, LANES), f32),
             VMEM((6, 400, LANES), f32),
@@ -736,23 +774,25 @@
             VMEM((400, 21 * LANES), bf16),
             VMEM((400, LANES), f32),
             VMEM((PEERS * PART, LANES), f32),
-            DMA((8,)),
-            DMA((3,)),
+            DMA((15,)),
+            DMA((4,)),
         ],
-    )(now, next_rows, far_in, near_in, top, wave, tables, radius)
+        limit=62 * 1024 * 1024,
+    )(forward_now, adjoint_now, next_rows, far_in, near_in, top, wave, tables, radius)
     arrived = lax.all_to_all(terms.reshape(PEERS, PART, LANES), FOURIER, 0, 0, tiled=True)
 
     forward_part, adjoint_part, edge = call(
         stress_kernel,
         "stress",
         8,
-        [HBM] * 8,
+        [HBM] * 10,
         (shape(3, 132, LANES), shape(3, 132, LANES), shape(6, 24, LANES)),
         [
             VMEM((PEERS * PART, LANES), f32),
-            VMEM((KIND_ROWS, LANES), bf16),
+            VMEM((3 * LANES, 7 * LANES), bf16),
+            VMEM((1, 3, 4, ROWS, LANES), f32),
             VMEM((13, 400, LANES), f32),
-            VMEM((BACK_ROWS, LANES), bf16),
+            VMEM((4 * LANES, 2 * LANES), bf16),
             VMEM((6, 132, LANES), f32),
             VMEM((6, 132, LANES), f32),
             VMEM((132, LANES), f32),
@@ -763,13 +803,15 @@
             VMEM((2, 6, 400, LANES), f32),
             VMEM((NODES, 8, LANES), f32),
             VMEM((4, 6, ROWS, LANES), f32),
-            DMA((9,)),
+            DMA((13,)),
             DMA((3,)),
         ],
         limit=62 * 1024 * 1024,
     )(
         gathered,
+        sample,
         tables,
+        samples,
         strain,
         forward_now,
         adjoint_now,

time: 66.2 us -> 63.5 us (0.959)
  waiting for transfers between devices: 12.8 us -> 8.65 us
  Pallas kernels: 21.6 us -> 19.3 us
  local copies, waits for them, and re-layouts: 3.95 us -> 6.23 us
  starting transfers between devices: 25.7 us -> 27.1 us
    all_to_all x1, waiting for transfers between devices: 2.59 us -> 0.01 us  [body(): lax.all_to_all(spread, FOURIER, 0, 0, tiled=True)]
    pallas_call x3, Pallas kernels: 17.8 us -> 15.6 us  [the longest x1 6.82 us: body(): call(strain_kernel, 'strain', 8, [HBM] * 9, (shape(3, 4, ROWS, LANES), sh...]
    ppermute x1, waiting for transfers between devices: 3.56 us -> 2 us  [body(): far_in = lax.ppermute(far, FOURIER, swaps(1))]
    slice x1 -> x2, local copies, waits for them, and re-layouts: 0.01 us -> 1.55 us  [the longest x1 0.78 us: body(): forward_now[:, :24]]
    all_to_all x1, starting transfers between devices: 6.43 us -> 7.46 us  [body(): lax.all_to_all(spread, FOURIER, 0, 0, tiled=True)]
    unnamed x5 -> x10, local copies, waits for them, and re-layouts: 0.96 us -> 1.94 us
    concatenate x1 -> x0, local copies, waits for them, and re-layouts: 0.95 us -> none  [body(): now = jnp.concatenate([forward_now, adjoint_now], axis=0)]
    broadcast_in_dim x2, local copies, waits for them, and re-layouts: 0.19 us -> 0.89 us  [body(): jnp.broadcast_to(jnp.transpose(inv_radius.reshape(16, NODES)).reshape(400...]
  transfers between devices with their start and end apart: 6 -> 6, of which waited for: 4 -> 2; matrix products, arithmetic and copies ran while one was open for 4% -> 6% of each run, Pallas kernels for 29% -> 28%
where the time goes in v2:
time: 63.5 us; the launch traced here: 62.8 us
  starting transfers between devices  27.1 us (43%)
  Pallas kernels  19.3 us (30%)
  waiting for transfers between devices  8.65 us (14%)
  local copies, waits for them, and re-layouts  6.23 us (10%)
  between operations  0.76 us (1%)
  other arithmetic  0.75 us (1%)
    all_to_all x1, starting transfers between devices, body(): lax.all_to_all(spread, FOURIER, 0, 0, tiled=True)  7.46 us
    pallas_call x1, Pallas kernels, body(): call(strain_kernel, 'strain', 8, [HBM] * 9, (shape(3, 4, ROWS, LANES), sh...  6.82 us
    all_to_all x1, starting transfers between devices, body(): lax.all_to_all(terms.reshape(PEERS, PART, LANES), FOURIER, 0, 0, tiled=True)  6.7 us
    ppermute x1, waiting for transfers between devices, body(): lax.ppermute(edge, MERIDIAN, [(s, s + 1) for s in range(slices - 1)])  6.64 us
    pallas_call x1, Pallas kernels, body(): call(stress_kernel, 'stress', 8, [HBM] * 10, (shape(3, 132, LANES), shape...  6.63 us
    ppermute x1, starting transfers between devices, body(): lax.ppermute(first_rows, MERIDIAN, [(s, s - 1) for s in range(1, slices)])  4.76 us
    ppermute x1, starting transfers between devices, body(): far_in = lax.ppermute(far, FOURIER, swaps(1))  4.33 us
    pallas_call x1, Pallas kernels, body(): call(pack_kernel, 'pack', 2, [HBM] * 3, (shape(*halo), shape(*halo), shap...  2.1 us
  transfers between devices with their start and end apart: 6, of which 2 were waited for; matrix products, arithmetic and copies ran while one was open for 6% of the time, Pallas kernels for 28%

profile of v2, /device:TPU:388, one launch (start us, length us, event | category | flops | bytes accessed | tf_op | source)
XLA Modules:
  0.0 62.8 jit_solution(5213753992934604574)
XLA Ops:
  0.6 0.8 %slice.12 = f32[3,24,128]{2,1,0:T(8,128)S(1)} slice(f32[3,132,128]{2,1,0:T(8,128)} %forward_hbm.5), slice={[0:3], [0:24], [0:128]} | slice | bytes 73728 | tf_op jit(solution)/shard_map/slice | solution.py:713
  1.4 0.8 %slice.13 = f32[3,24,128]{2,1,0:T(8,128)S(1)} slice(f32[3,132,128]{2,1,0:T(8,128)} %adjoint_hbm.5), slice={[0:3], [0:24], [0:128]} | slice | bytes 73728 | tf_op jit(solution)/shard_map/slice | solution.py:713
  2.2 4.8 %collective-permute-start = (f32[6,24,128]{2,1,0:T(8,128)S(1)}, f32[6,24,128]{2,1,0:T(8,128)S(1)}, u32[]{:S(2)}, u32[]{:S(2)}) collective-permute-start(f32[6,24,128]{2,1,0:T(8,128)S(1)} %pad_maximum_fusion), channel_id=1, source_target_pairs={{1,0},{2,1},{3,2},{4,3},{5,4},{6,5},{7,6},{8,7},{9,8},{10,9},{11,1... | collective-permute-start | bytes 221192 | tf_op jit(solution)/shard_map/ppermute | solution.py:730
  7.0 2.0 %spread.1 = f32[16,80,128]{2,1,0:T(8,128)} custom-call(f32[21,17,1,25]{3,2,1,0:T(1,128)} %moduli_hbm), custom_call_target="tpu_custom_call" | custom-call | flops 4000000 | bytes 12000000 | tf_op jit(solution)/shard_map/spread/pallas_call | solution.py:715
  9.0 7.5 %all-to-all-start = ((f32[16,80,128]{2,1,0:T(8,128)}), f32[16,80,128]{2,1,0:T(8,128)S(1)}, u32[]{:S(2)}, u32[]{:S(2)}) async-start(f32[16,80,128]{2,1,0:T(8,128)} %spread.1), calls=%async_computation | async-start | bytes 1310720 | tf_op jit(solution)/shard_map/all_to_all | solution.py:729
  16.5 0.8 %reshape.21 = f32[132,2]{1,0:T(8,128)S(1)} reshape(f32[264]{0:T(512)} %param.16) | data formatting | bytes 2112 | tf_op jit(solution)/shard_map/reshape | solution.py:732
  17.3 0.2 slice_reduce_fusion.1
  17.5 0.7 %fusion.mass_hbm = f32[132,128]{1,0:T(8,128)} fusion(f32[132]{0:T(256)S(1)} %get-tuple-element.38, f32[132]{0:T(256)S(1)} %get-tuple-element.37, s32[128]{0:T(128)S(1)} %get-tuple-element.39, s32[128]{0:T(128)S(1)} %get-tuple-element.40, pred[128]{0:T(512)(128)(4,1)S(1)} %compare_and_fusion), kind=kLoop, calls=%fused_computation.4 | loop fusion | flops 50688 | bytes 69792 | tf_op jit(solution)/shard_map/jit(_where)/select_n | solution.py:734
  18.2 0.0 collective-permute-done.next_hbm
  18.2 0.0 copy-start.2
  18.2 0.6 %copy-done.2 = f32[6,24,128]{2,1,0:T(8,128)} copy-done((f32[6,24,128]{2,1,0:T(8,128)}, f32[6,24,128]{2,1,0:T(8,128)S(1)}, u32[]{:S(2)}) %copy-start.2) | copy-done | bytes 73752
  18.9 2.1 %pack.1 = (f32[6,40,128]{2,1,0:T(8,128)}, f32[6,40,128]{2,1,0:T(8,128)}, f32[6,40,128]{2,1,0:T(8,128)}) custom-call(f32[3,132,128]{2,1,0:T(8,128)} %forward_hbm.5, f32[3,132,128]{2,1,0:T(8,128)} %adjoint_hbm.5, f32[6,24,128]{2,1,0:T(8,128)} %copy-done.2), custom_call_target="tpu_custom_call" | custom-call | flops 2000000 | bytes 6000000 | tf_op jit(solution)/shard_map/pack/pallas_call | solution.py:736
  21.0 4.3 %collective-permute-start.1 = (f32[6,40,128]{2,1,0:T(8,128)}, f32[6,40,128]{2,1,0:T(8,128)S(1)}, u32[]{:S(2)}, u32[]{:S(2)}) collective-permute-start(f32[6,40,128]{2,1,0:T(8,128)} %get-tuple-element.23), channel_id=1, source_target_pairs={{32,64},{64,32},{96,128},{128,96},{160,192},{192,160},{224,256},{2... | collective-permute-start | bytes 368648 | tf_op jit(solution)/shard_map/ppermute | solution.py:745
  25.3 1.9 %collective-permute-start.2 = (f32[6,40,128]{2,1,0:T(8,128)}, f32[6,40,128]{2,1,0:T(8,128)S(1)}, u32[]{:S(2)}, u32[]{:S(2)}) collective-permute-start(f32[6,40,128]{2,1,0:T(8,128)} %get-tuple-element.24), channel_id=1, source_target_pairs={{0,32},{32,0},{64,96},{96,64},{128,160},{160,128},{192,224},{224,1... | collective-permute-start | bytes 368648 | tf_op jit(solution)/shard_map/ppermute | solution.py:746
  27.3 0.8 %reshape.22 = f32[16,25]{1,0:T(8,128)S(1)} reshape(f32[400]{0:T(512)} %param.15) | data formatting | bytes 3200 | tf_op jit(solution)/shard_map/reshape | solution.py:749
  28.0 0.1 copy.15
  28.1 0.1 broadcast_in_dim.31
  28.2 0.8 %broadcast_in_dim.32.radius_hbm = f32[400,128]{1,0:T(8,128)} broadcast(f32[400]{0:T(512)S(1)} %broadcast_in_dim.31), dimensions={0} | broadcast | bytes 206400 | tf_op jit(solution)/shard_map/broadcast_in_dim | solution.py:748
  29.0 2.0 %collective-permute-done.1.far_hbm = f32[6,40,128]{2,1,0:T(8,128)S(1)} collective-permute-done((f32[6,40,128]{2,1,0:T(8,128)}, f32[6,40,128]{2,1,0:T(8,128)S(1)}, u32[]{:S(2)}, u32[]{:S(2)}) %collective-permute-start.1) | collective-permute-done | bytes 122912 | tf_op jit(solution)/shard_map/ppermute | solution.py:745
  31.0 0.0 copy-start.3
  31.0 0.0 collective-permute-done.2.near_hbm
  31.0 0.6 %copy-done.3 = f32[6,40,128]{2,1,0:T(8,128)} copy-done((f32[6,40,128]{2,1,0:T(8,128)}, f32[6,40,128]{2,1,0:T(8,128)S(1)}, u32[]{:S(2)}) %copy-start.3) | copy-done | bytes 122904
  31.7 0.0 copy-start.4
  31.7 0.6 %copy-done.4 = f32[6,40,128]{2,1,0:T(8,128)} copy-done((f32[6,40,128]{2,1,0:T(8,128)}, f32[6,40,128]{2,1,0:T(8,128)S(1)}, u32[]{:S(2)}) %copy-start.4) | copy-done | bytes 122904
  32.3 6.8 %strain.1 = (f32[3,4,160,128]{3,2,1,0:T(8,128)}, f32[7,400,128]{2,1,0:T(8,128)}, f32[1280,128]{1,0:T(8,128)}) custom-call(f32[3,132,128]{2,1,0:T(8,128)} %forward_hbm.5, f32[3,132,128]{2,1,0:T(8,128)} %adjoint_hbm.5, f32[6,24,128]{2,1,0:T(8,128)} %copy-done.2, f32[6,40,128]{2,1,0:T(8,128)} %copy-done.3, f32[6,40,128]{2,1,0:T(8,128)} %copy-done.4, ...), custom_call_target="tpu_custom_call" | custom-call | flops 8000000 | bytes 24000000 | tf_op jit(solution)/shard_map/strain/pallas_call | solution.py:752
  39.1 0.0 all-to-all-done
  39.1 0.0 copy-start.1
  39.2 6.7 %all-to-all-start.1 = ((f32[16,80,128]{2,1,0:T(8,128)}), f32[16,80,128]{2,1,0:T(8,128)S(1)}, u32[]{:S(2)}, u32[]{:S(2)}) async-start(f32[16,80,128]{2,1,0:T(8,128)} %bitcast.4), calls=%async_computation.1 | async-start | bytes 1310720 | tf_op jit(solution)/shard_map/all_to_all | solution.py:782
  45.9 0.0 copy-start
  45.9 0.0 copy-done.1
  45.9 6.6 %stress.1 = (f32[3,132,128]{2,1,0:T(8,128)}, f32[3,132,128]{2,1,0:T(8,128)}, f32[6,24,128]{2,1,0:T(8,128)}) custom-call(f32[1280,128]{1,0:T(8,128)} %bitcast.3, bf16[2,2,128,896]{3,2,1,0:T(8,128)(2,1)} %constant.25.clone.sample_hbm, bf16[19968,128]{1,0:T(8,128)(2,1)} %constant.24.clone.table_hbm, f32[3,4,160,128]{3,2,1,0:T(8,128)} %get-tuple-element.30.forward_samples_hbm, ...), custom_call_target="tpu_custom_call" | custom-call | flops 8000000 | bytes 24000000 | tf_op jit(solution)/shard_map/stress/pallas_call | solution.py:784
  52.5 1.9 %collective-permute-start.3 = (f32[6,24,128]{2,1,0:T(8,128)}, f32[6,24,128]{2,1,0:T(8,128)S(1)}, u32[]{:S(2)}, u32[]{:S(2)}) collective-permute-start(f32[6,24,128]{2,1,0:T(8,128)} %get-tuple-element.35), channel_id=1, source_target_pairs={{0,1},{1,2},{2,3},{3,4},{4,5},{5,6},{6,7},{7,8},{8,9},{9,10},{10,1... | collective-permute-start | bytes 221192 | tf_op jit(solution)/shard_map/ppermute | solution.py:822
  54.4 6.6 %collective-permute-done.3.edge_hbm = f32[6,24,128]{2,1,0:T(8,128)S(1)} collective-permute-done((f32[6,24,128]{2,1,0:T(8,128)}, f32[6,24,128]{2,1,0:T(8,128)S(1)}, u32[]{:S(2)}, u32[]{:S(2)}) %collective-permute-start.3) | collective-permute-done | bytes 73760 | tf_op jit(solution)/shard_map/ppermute | solution.py:822
  61.1 0.0 all-to-all-done.1.terms_hbm
  61.1 0.0 copy-done
  61.1 1.7 %finish.1 = (f32[3,132,128]{2,1,0:T(8,128)}, f32[3,132,128]{2,1,0:T(8,128)}, f32[21,17,1,25]{3,2,1,0:T(1,128)}) custom-call(f32[3,132,128]{2,1,0:T(8,128)} %get-tuple-element.33.forward_hbm, f32[3,132,128]{2,1,0:T(8,128)} %get-tuple-element.34.adjoint_hbm, ...), custom_call_target="tpu_custom_call", output_to_operand_aliasing={{0}: (0, {}), {1}: (1, {})} | custom-call | flops 2000000 | bytes 6000000 | tf_op jit(solution)/shard_map/finish/pallas_call | solution.py:823
  (3 shorter events, 0.0 us)
Async XLA Ops:
  2.2 16.0 %collective-permute-start = (f32[6,24,128]{2,1,0:T(8,128)S(1)}, f32[6,24,128]{2,1,0:T(8,128)S(1)}, u32[]{:S(2)}, u32[]{:S(2)}) collective-permute-start(f32[6,24,128]{2,1,0:T(8,128)S(1)} %pad_maximum_fusion), channel_id=1, source_target_pairs={{1,0},{2,1},{3,2},{4,3},{5,4},{6,5},{7,6},{8,7},{9,8},{10,9},{11,1... | collective-permute-start | bytes 221192 | tf_op jit(solution)/shard_map/ppermute | solution.py:730
  9.0 30.1 %all-to-all-start = ((f32[16,80,128]{2,1,0:T(8,128)}), f32[16,80,128]{2,1,0:T(8,128)S(1)}, u32[]{:S(2)}, u32[]{:S(2)}) async-start(f32[16,80,128]{2,1,0:T(8,128)} %spread.1), calls=%async_computation | async-start | bytes 1310720 | tf_op jit(solution)/shard_map/all_to_all | solution.py:729
  18.2 0.6 %copy-start.2 = (f32[6,24,128]{2,1,0:T(8,128)}, f32[6,24,128]{2,1,0:T(8,128)S(1)}, u32[]{:S(2)}) copy-start(f32[6,24,128]{2,1,0:T(8,128)S(1)} %collective-permute-done.next_hbm) | copy-start | bytes 221188
  21.0 10.0 %collective-permute-start.1 = (f32[6,40,128]{2,1,0:T(8,128)}, f32[6,40,128]{2,1,0:T(8,128)S(1)}, u32[]{:S(2)}, u32[]{:S(2)}) collective-permute-start(f32[6,40,128]{2,1,0:T(8,128)} %get-tuple-element.23), channel_id=1, source_target_pairs={{32,64},{64,32},{96,128},{128,96},{160,192},{192,160},{224,256},{2... | collective-permute-start | bytes 368648 | tf_op jit(solution)/shard_map/ppermute | solution.py:745
  25.3 5.7 %collective-permute-start.2 = (f32[6,40,128]{2,1,0:T(8,128)}, f32[6,40,128]{2,1,0:T(8,128)S(1)}, u32[]{:S(2)}, u32[]{:S(2)}) collective-permute-start(f32[6,40,128]{2,1,0:T(8,128)} %get-tuple-element.24), channel_id=1, source_target_pairs={{0,32},{32,0},{64,96},{96,64},{128,160},{160,128},{192,224},{224,1... | collective-permute-start | bytes 368648 | tf_op jit(solution)/shard_map/ppermute | solution.py:746
  31.0 0.6 %copy-start.3 = (f32[6,40,128]{2,1,0:T(8,128)}, f32[6,40,128]{2,1,0:T(8,128)S(1)}, u32[]{:S(2)}) copy-start(f32[6,40,128]{2,1,0:T(8,128)S(1)} %collective-permute-done.1.far_hbm) | copy-start | bytes 368644
  31.7 0.6 %copy-start.4 = (f32[6,40,128]{2,1,0:T(8,128)}, f32[6,40,128]{2,1,0:T(8,128)S(1)}, u32[]{:S(2)}) copy-start(f32[6,40,128]{2,1,0:T(8,128)S(1)} %collective-permute-done.2.near_hbm) | copy-start | bytes 368644
  39.1 6.7 %copy-start.1 = (f32[16,80,128]{2,1,0:T(8,128)}, f32[16,80,128]{2,1,0:T(8,128)S(1)}, u32[]{:S(2)}) copy-start(f32[16,80,128]{2,1,0:T(8,128)S(1)} %all-to-all-done) | copy-start | bytes 1966084
  39.2 21.9 %all-to-all-start.1 = ((f32[16,80,128]{2,1,0:T(8,128)}), f32[16,80,128]{2,1,0:T(8,128)S(1)}, u32[]{:S(2)}, u32[]{:S(2)}) async-start(f32[16,80,128]{2,1,0:T(8,128)} %bitcast.4), calls=%async_computation.1 | async-start | bytes 1310720 | tf_op jit(solution)/shard_map/all_to_all | solution.py:782
  45.9 15.2 %copy-start = (f32[132,128]{1,0:T(8,128)S(1)}, f32[132,128]{1,0:T(8,128)}, u32[]{:S(2)}) copy-start(f32[132,128]{1,0:T(8,128)} %fusion.mass_hbm) | copy-start | bytes 202756
  52.5 8.6 %collective-permute-start.3 = (f32[6,24,128]{2,1,0:T(8,128)}, f32[6,24,128]{2,1,0:T(8,128)S(1)}, u32[]{:S(2)}, u32[]{:S(2)}) collective-permute-start(f32[6,24,128]{2,1,0:T(8,128)} %get-tuple-element.35), channel_id=1, source_target_pairs={{0,1},{1,2},{2,3},{3,4},{4,5},{5,6},{6,7},{7,8},{8,9},{9,10},{10,1... | collective-permute-start | bytes 221192 | tf_op jit(solution)/shard_map/ppermute | solution.py:822

commit v3 on v2

--- a/solution.py
+++ b/solution.py
@@ -248,6 +248,33 @@
     return copies
 
 
+def radius_rows(line_ref):
+    row = lax.broadcasted_iota(jnp.int32, (400, 400), 0)
+    source = lax.broadcasted_iota(jnp.int32, (400, 400), 1)
+    place = (row & 15) * NODES + lax.shift_right_logical(row, 4)
+    chosen = jnp.where(place == source, line_ref[...][None, :], 0.0)
+    return jnp.dot(
+        chosen,
+        jnp.ones((400, LANES), f32),
+        precision=lax.Precision.HIGHEST,
+        preferred_element_type=f32,
+    )
+
+
+def mass_rows(line_ref, rows):
+    row = lax.broadcasted_iota(jnp.int32, (rows, 264), 0)
+    source = lax.broadcasted_iota(jnp.int32, (rows, 264), 1)
+    chosen = jnp.where(lax.shift_right_logical(source, 1) == row, line_ref[...][None, :], 0.0)
+    parity = lax.broadcasted_iota(jnp.int32, (264, LANES), 0) & 1
+    lane = lax.broadcasted_iota(jnp.int32, (264, LANES), 1) & 1
+    return jnp.dot(
+        chosen,
+        jnp.where(parity == lane, 1.0, 0.0).astype(f32),
+        precision=lax.Precision.HIGHEST,
+        preferred_element_type=f32,
+    )
+
+
 def spread_kernel(moduli_hbm, spread_hbm, moduli_ref, part_ref, sems, out_sems):
     (moduli_copy,) = started(sems, ((moduli_hbm, moduli_ref),))
     part_ref[72:PART, :] = jnp.zeros((PART - 72, LANES), f32)
@@ -374,6 +401,7 @@
     top_ref,
     wave,
     project,
+    radius_line,
     radius_ref,
     strain_ref,
     halo_ref,
@@ -396,7 +424,7 @@
             (forward_hbm, x_ref.at[0:3, 0:132, :]),
             (adjoint_hbm, x_ref.at[3:6, 0:132, :]),
             (next_hbm, x_ref.at[:, NEXT:ROWS, :]),
-            (radius_hbm, radius_ref),
+            (radius_hbm, radius_line),
         )
         + tuple(
             (wave_hbm.at[f_at, part], wave.at[k * LANES : (k + 1) * LANES, :])
@@ -415,6 +443,8 @@
         ),
     )
     x_ref[:, 132:NEXT, :] = jnp.zeros((6, NEXT - 132, LANES), f32)
+    copies[6].wait()
+    radius_ref[...] = radius_rows(radius_line)
     for copy in copies[:3]:
         copy.wait()
     group = lax.broadcasted_iota(jnp.int32, (CHUNK, LANES), 1) // 32
@@ -426,7 +456,7 @@
             d = top if g == 2 else pltpu.roll(top, (64 - 32 * g) % LANES, 1)
             rows = jnp.where(group == 0, a, jnp.where(group == 1, b, d))
             halo_ref[c, CHUNK * g : CHUNK * g + CHUNK, :] = jnp.where(group == 3, 0.0, rows)
-    for copy in copies[3:13]:
+    for copy in copies[3:6] + copies[7:13]:
         copy.wait()
     radius_copy = pltpu.make_async_copy(radius_ref, strain_hbm.at[6], out_sems.at[2])
     radius_copy.start()
@@ -504,7 +534,7 @@
     back,
     now_ref,
     last_ref,
-    mass_ref,
+    mass_line,
     out_ref,
     edge_ref,
     order_ref,
@@ -538,7 +568,7 @@
             (adjoint_hbm, now_ref.at[3:6]),
             (forward_last_hbm, last_ref.at[0:3]),
             (adjoint_last_hbm, last_ref.at[3:6]),
-            (mass_hbm, mass_ref),
+            (mass_hbm, mass_line),
         ),
     )
     grid_ref[...] = jnp.zeros(grid_ref.shape, f32)
@@ -601,7 +631,7 @@
 
     for copy in copies[6:]:
         copy.wait()
-    mass = mass_ref[...]
+    mass = mass_rows(mass_line, 132)
     for c in range(6):
         joined = jnp.concatenate([grid_ref[k, c] for k in range(4)], axis=1)
         force = beside(*halves(joined), back[...])
@@ -629,7 +659,7 @@
     kernel_hbm,
     rows,
     edge_ref,
-    mass_ref,
+    mass_line,
     terms_ref,
     kernel_ref,
     sems,
@@ -641,13 +671,13 @@
             (forward_hbm.at[:, 0:24, :], rows.at[0:3]),
             (adjoint_hbm.at[:, 0:24, :], rows.at[3:6]),
             (edge_hbm, edge_ref),
-            (mass_hbm.at[0:24, :], mass_ref),
+            (mass_hbm, mass_line),
             (terms_hbm, terms_ref),
         ),
     )
     for copy in copies[:4]:
         copy.wait()
-    mass = mass_ref[...]
+    mass = mass_rows(mass_line, 24)
     for c in range(6):
         rows[c] = rows[c] - mass * edge_ref[c]
     copies[4].wait()
@@ -726,13 +756,10 @@
         ],
         limit=62 * 1024 * 1024,
     )(moduli)[0]
+    next_rows = lax.ppermute(first_rows, MERIDIAN, [(s, s - 1) for s in range(1, slices)])
+    spread, next_rows = lax.optimization_barrier((spread, next_rows))
     gathered = lax.all_to_all(spread, FOURIER, 0, 0, tiled=True).reshape(PEERS * PART, LANES)
-    next_rows = lax.ppermute(first_rows, MERIDIAN, [(s, s - 1) for s in range(1, slices)])
-
-    pair = inv_mass.reshape(132, 2)
-    even = lax.broadcasted_iota(jnp.int32, (132, LANES), 1) % 2 == 0
-    mass = jnp.where(even, pair[:, 0:1], pair[:, 1:2])
-    next_rows, mass = lax.optimization_barrier((next_rows, mass))
+
     far, near, top = call(
         pack_kernel,
         "pack",
@@ -744,11 +771,6 @@
     )(forward_now, adjoint_now, next_rows)
     far_in = lax.ppermute(far, FOURIER, swaps(1))
     near_in = lax.ppermute(near, FOURIER, swaps(0))
-    inv_radius, top = lax.optimization_barrier((inv_radius, top))
-    radius = jnp.broadcast_to(
-        jnp.transpose(inv_radius.reshape(16, NODES)).reshape(400, 1), (400, LANES)
-    )
-    radius, mass = lax.optimization_barrier((radius, mass))
     samples, strain, terms = call(
         strain_kernel,
         "strain",
@@ -765,6 +787,7 @@
             VMEM(halo, f32),
             VMEM((6 * LANES, 4 * LANES), bf16),
             VMEM((7 * LANES, 2 * LANES), bf16),
+            VMEM((400,), f32),
             VMEM((400, LANES), f32),
             VMEM((6, 400, LANES), f32),
             VMEM((6, ROWS, LANES), f32),
@@ -778,7 +801,7 @@
             DMA((4,)),
         ],
         limit=62 * 1024 * 1024,
-    )(forward_now, adjoint_now, next_rows, far_in, near_in, top, wave, tables, radius)
+    )(forward_now, adjoint_now, next_rows, far_in, near_in, top, wave, tables, inv_radius)
     arrived = lax.all_to_all(terms.reshape(PEERS, PART, LANES), FOURIER, 0, 0, tiled=True)
 
     forward_part, adjoint_part, edge = call(
@@ -795,7 +818,7 @@
             VMEM((4 * LANES, 2 * LANES), bf16),
             VMEM((6, 132, LANES), f32),
             VMEM((6, 132, LANES), f32),
-            VMEM((132, LANES), f32),
+            VMEM((264,), f32),
             VMEM((6, 132, LANES), f32),
             VMEM((6, 24, LANES), f32),
             VMEM((400, LANES), f32),
@@ -817,7 +840,7 @@
         adjoint_now,
         forward_last,
         adjoint_last,
-        mass,
+        inv_mass,
     )
     carried = lax.ppermute(edge, MERIDIAN, [(s, s + 1) for s in range(slices - 1)])
     return call(
@@ -829,14 +852,14 @@
         [
             VMEM((6, 24, LANES), f32),
             VMEM((6, 24, LANES), f32),
-            VMEM((24, LANES), f32),
+            VMEM((264,), f32),
             VMEM((PEERS, PART, LANES), f32),
             VMEM((21, 17, 1, NODES), f32),
             DMA((5,)),
             DMA((3,)),
         ],
         {0: 0, 1: 1},
-    )(forward_part, adjoint_part, carried, mass, arrived)
+    )(forward_part, adjoint_part, carried, inv_mass, arrived)
 
 
 def solution(mesh):

time: 63.5 us -> 63 us (level)
  local copies, waits for them, and re-layouts: 6.23 us -> 2.24 us
  Pallas kernels: 19.3 us -> 21.4 us
  starting transfers between devices: 27.1 us -> 28.5 us
  waiting for transfers between devices: 8.65 us -> 9.47 us
  other arithmetic: 0.75 us -> 0.01 us
    ppermute x1, waiting for transfers between devices: 2 us -> 3.82 us  [body(): far_in = lax.ppermute(far, FOURIER, swaps(1))]
    pallas_call x1, Pallas kernels: 6.82 us -> 8.53 us  [body(): call(strain_kernel, 'strain', 8, [HBM] * 9, (shape(3, 4, ROWS, LANES), sh...]
    reshape x2 -> x0, local copies, waits for them, and re-layouts: 1.58 us -> none  [the longest x1 0.82 us: body(): pair = inv_mass.reshape(132, 2)]
    ppermute x1, starting transfers between devices: 1.92 us -> 3.4 us  [body(): lax.ppermute(edge, MERIDIAN, [(s, s + 1) for s in range(slices - 1)])]
    unnamed x10, local copies, waits for them, and re-layouts: 1.94 us -> 0.7 us
    ppermute x1, waiting for transfers between devices: 6.64 us -> 5.64 us  [body(): lax.ppermute(edge, MERIDIAN, [(s, s + 1) for s in range(slices - 1)])]
    broadcast_in_dim x2 -> x0, local copies, waits for them, and re-layouts: 0.89 us -> none  [body(): jnp.broadcast_to(jnp.transpose(inv_radius.reshape(16, NODES)).reshape(400...]
    select_n x1 -> x0, other arithmetic: 0.73 us -> none  [body(): mass = jnp.where(even, pair[:, 0:1], pair[:, 1:2])]
  transfers between devices with their start and end apart: 6 -> 6, of which waited for: 2 -> 2; matrix products, arithmetic and copies ran while one was open for 6% -> 0% of each run, Pallas kernels for 28% -> 31%
where the time goes in v3:
time: 63 us; the launch traced here: 62.4 us
  starting transfers between devices  28.5 us (45%)
  Pallas kernels  21.4 us (34%)
  waiting for transfers between devices  9.47 us (15%)
  local copies, waits for them, and re-layouts  2.24 us (4%)
  between operations  0.75 us (1%)
    pallas_call x1, Pallas kernels, body(): call(strain_kernel, 'strain', 8, [HBM] * 9, (shape(3, 4, ROWS, LANES), sh...  8.53 us
    all_to_all x1, starting transfers between devices, body(): lax.all_to_all(spread, FOURIER, 0, 0, tiled=True)  7.46 us
    pallas_call x1, Pallas kernels, body(): call(stress_kernel, 'stress', 8, [HBM] * 10, (shape(3, 132, LANES), shape...  6.77 us
    all_to_all x1, starting transfers between devices, body(): lax.all_to_all(terms.reshape(PEERS, PART, LANES), FOURIER, 0, 0, tiled=True)  6.63 us
    ppermute x1, waiting for transfers between devices, body(): lax.ppermute(edge, MERIDIAN, [(s, s + 1) for s in range(slices - 1)])  5.64 us
    ppermute x1, starting transfers between devices, body(): lax.ppermute(first_rows, MERIDIAN, [(s, s - 1) for s in range(1, slices)])  4.76 us
    ppermute x1, starting transfers between devices, body(): far_in = lax.ppermute(far, FOURIER, swaps(1))  4.33 us
    ppermute x1, waiting for transfers between devices, body(): far_in = lax.ppermute(far, FOURIER, swaps(1))  3.82 us
  transfers between devices with their start and end apart: 6, of which 2 were waited for; matrix products, arithmetic and copies ran while one was open for 0% of the time, Pallas kernels for 31%

profile of v3, /device:TPU:388, one launch (start us, length us, event | category | flops | bytes accessed | tf_op | source)
XLA Modules:
  0.0 62.4 jit_solution(3102704739021730381)
XLA Ops:
  0.6 0.8 %slice.6 = f32[3,24,128]{2,1,0:T(8,128)S(1)} slice(f32[3,132,128]{2,1,0:T(8,128)} %forward_hbm.5), slice={[0:3], [0:24], [0:128]} | slice | bytes 73728 | tf_op jit(solution)/shard_map/slice | solution.py:743
  1.4 0.8 %slice.7 = f32[3,24,128]{2,1,0:T(8,128)S(1)} slice(f32[3,132,128]{2,1,0:T(8,128)} %adjoint_hbm.5), slice={[0:3], [0:24], [0:128]} | slice | bytes 73728 | tf_op jit(solution)/shard_map/slice | solution.py:743
  2.2 4.8 %collective-permute-start = (f32[6,24,128]{2,1,0:T(8,128)S(1)}, f32[6,24,128]{2,1,0:T(8,128)S(1)}, u32[]{:S(2)}, u32[]{:S(2)}) collective-permute-start(f32[6,24,128]{2,1,0:T(8,128)S(1)} %pad_maximum_fusion), channel_id=1, source_target_pairs={{1,0},{2,1},{3,2},{4,3},{5,4},{6,5},{7,6},{8,7},{9,8},{10,9},{11,1... | collective-permute-start | bytes 221192 | tf_op jit(solution)/shard_map/ppermute | solution.py:759
  7.0 2.0 %spread.1 = f32[16,80,128]{2,1,0:T(8,128)} custom-call(f32[21,17,1,25]{3,2,1,0:T(1,128)} %moduli_hbm), custom_call_target="tpu_custom_call" | custom-call | flops 4000000 | bytes 12000000 | tf_op jit(solution)/shard_map/spread/pallas_call | solution.py:745
  9.0 0.0 collective-permute-done.next_hbm
  9.0 0.0 copy-start.2
  9.0 7.5 %all-to-all-start = ((f32[16,80,128]{2,1,0:T(8,128)}), f32[16,80,128]{2,1,0:T(8,128)S(1)}, u32[]{:S(2)}, u32[]{:S(2)}) async-start(f32[16,80,128]{2,1,0:T(8,128)} %spread.1), calls=%async_computation | async-start | bytes 1310720 | tf_op jit(solution)/shard_map/all_to_all | solution.py:761
  16.5 0.0 copy-done.2
  16.5 2.1 %pack.1 = (f32[6,40,128]{2,1,0:T(8,128)}, f32[6,40,128]{2,1,0:T(8,128)}, f32[6,40,128]{2,1,0:T(8,128)}) custom-call(f32[3,132,128]{2,1,0:T(8,128)} %forward_hbm.5, f32[3,132,128]{2,1,0:T(8,128)} %adjoint_hbm.5, f32[6,24,128]{2,1,0:T(8,128)} %copy-done.2), custom_call_target="tpu_custom_call" | custom-call | flops 2000000 | bytes 6000000 | tf_op jit(solution)/shard_map/pack/pallas_call | solution.py:763
  18.6 4.3 %collective-permute-start.1 = (f32[6,40,128]{2,1,0:T(8,128)}, f32[6,40,128]{2,1,0:T(8,128)S(1)}, u32[]{:S(2)}, u32[]{:S(2)}) collective-permute-start(f32[6,40,128]{2,1,0:T(8,128)} %get-tuple-element.20), channel_id=1, source_target_pairs={{32,64},{64,32},{96,128},{128,96},{160,192},{192,160},{224,256},{2... | collective-permute-start | bytes 368648 | tf_op jit(solution)/shard_map/ppermute | solution.py:772
  23.0 1.9 %collective-permute-start.2 = (f32[6,40,128]{2,1,0:T(8,128)}, f32[6,40,128]{2,1,0:T(8,128)S(1)}, u32[]{:S(2)}, u32[]{:S(2)}) collective-permute-start(f32[6,40,128]{2,1,0:T(8,128)} %get-tuple-element.21), channel_id=1, source_target_pairs={{0,32},{32,0},{64,96},{96,64},{128,160},{160,128},{192,224},{224,1... | collective-permute-start | bytes 368648 | tf_op jit(solution)/shard_map/ppermute | solution.py:773
  24.9 3.8 %collective-permute-done.1.far_hbm = f32[6,40,128]{2,1,0:T(8,128)S(1)} collective-permute-done((f32[6,40,128]{2,1,0:T(8,128)}, f32[6,40,128]{2,1,0:T(8,128)S(1)}, u32[]{:S(2)}, u32[]{:S(2)}) %collective-permute-start.1) | collective-permute-done | bytes 122912 | tf_op jit(solution)/shard_map/ppermute | solution.py:772
  28.7 0.0 copy-start.3
  28.7 0.0 collective-permute-done.2.near_hbm
  28.7 0.0 copy-start.4
  28.7 0.6 %copy-done.3 = f32[6,40,128]{2,1,0:T(8,128)} copy-done((f32[6,40,128]{2,1,0:T(8,128)}, f32[6,40,128]{2,1,0:T(8,128)S(1)}, u32[]{:S(2)}) %copy-start.3) | copy-done | bytes 122904
  29.4 0.0 copy-done.4
  29.4 8.5 %strain.1 = (f32[3,4,160,128]{3,2,1,0:T(8,128)}, f32[7,400,128]{2,1,0:T(8,128)}, f32[1280,128]{1,0:T(8,128)}) custom-call(f32[3,132,128]{2,1,0:T(8,128)} %forward_hbm.5, f32[3,132,128]{2,1,0:T(8,128)} %adjoint_hbm.5, f32[6,24,128]{2,1,0:T(8,128)} %copy-done.2, f32[6,40,128]{2,1,0:T(8,128)} %copy-done.3, f32[6,40,128]{2,1,0:T(8,128)} %copy-done.4, ...), custom_call_target="tpu_custom_call" | custom-call | flops 8000000 | bytes 24000000 | tf_op jit(solution)/shard_map/strain/pallas_call | solution.py:774
  37.9 0.0 all-to-all-done
  37.9 0.0 copy-start.1
  38.0 6.6 %all-to-all-start.1 = ((f32[16,80,128]{2,1,0:T(8,128)}), f32[16,80,128]{2,1,0:T(8,128)S(1)}, u32[]{:S(2)}, u32[]{:S(2)}) async-start(f32[16,80,128]{2,1,0:T(8,128)} %bitcast.3), calls=%async_computation.1 | async-start | bytes 1310720 | tf_op jit(solution)/shard_map/all_to_all | solution.py:805
  44.6 0.0 copy-start
  44.6 0.0 copy-done.1
  44.6 6.8 %stress.1 = (f32[3,132,128]{2,1,0:T(8,128)}, f32[3,132,128]{2,1,0:T(8,128)}, f32[6,24,128]{2,1,0:T(8,128)}) custom-call(f32[1280,128]{1,0:T(8,128)} %bitcast.2, bf16[2,2,128,896]{3,2,1,0:T(8,128)(2,1)} %constant.8.clone.sample_hbm, bf16[19968,128]{1,0:T(8,128)(2,1)} %constant.7.clone.table_hbm, f32[3,4,160,128]{3,2,1,0:T(8,128)} %get-tuple-element.23.forward_samples_hbm, ...), custom_call_target="tpu_custom_call" | custom-call | flops 8000000 | bytes 24000000 | tf_op jit(solution)/shard_map/stress/pallas_call | solution.py:807
  51.4 3.4 %collective-permute-start.3 = (f32[6,24,128]{2,1,0:T(8,128)}, f32[6,24,128]{2,1,0:T(8,128)S(1)}, u32[]{:S(2)}, u32[]{:S(2)}) collective-permute-start(f32[6,24,128]{2,1,0:T(8,128)} %get-tuple-element.27), channel_id=1, source_target_pairs={{0,1},{1,2},{2,3},{3,4},{4,5},{5,6},{6,7},{7,8},{8,9},{9,10},{10,1... | collective-permute-start | bytes 221192 | tf_op jit(solution)/shard_map/ppermute | solution.py:845
  54.8 5.6 %collective-permute-done.3.edge_hbm = f32[6,24,128]{2,1,0:T(8,128)S(1)} collective-permute-done((f32[6,24,128]{2,1,0:T(8,128)}, f32[6,24,128]{2,1,0:T(8,128)S(1)}, u32[]{:S(2)}, u32[]{:S(2)}) %collective-permute-start.3) | collective-permute-done | bytes 73760 | tf_op jit(solution)/shard_map/ppermute | solution.py:845
  60.4 0.0 all-to-all-done.1.terms_hbm
  60.4 0.0 copy-done
  60.4 1.9 %finish.1 = (f32[3,132,128]{2,1,0:T(8,128)}, f32[3,132,128]{2,1,0:T(8,128)}, f32[21,17,1,25]{3,2,1,0:T(1,128)}) custom-call(f32[3,132,128]{2,1,0:T(8,128)} %get-tuple-element.25.forward_hbm, f32[3,132,128]{2,1,0:T(8,128)} %get-tuple-element.26.adjoint_hbm, ...), custom_call_target="tpu_custom_call", output_to_operand_aliasing={{0}: (0, {}), {1}: (1, {})} | custom-call | flops 2000000 | bytes 6000000 | tf_op jit(solution)/shard_map/finish/pallas_call | solution.py:846
  (1 shorter events, 0.0 us)
Async XLA Ops:
  2.2 6.8 %collective-permute-start = (f32[6,24,128]{2,1,0:T(8,128)S(1)}, f32[6,24,128]{2,1,0:T(8,128)S(1)}, u32[]{:S(2)}, u32[]{:S(2)}) collective-permute-start(f32[6,24,128]{2,1,0:T(8,128)S(1)} %pad_maximum_fusion), channel_id=1, source_target_pairs={{1,0},{2,1},{3,2},{4,3},{5,4},{6,5},{7,6},{8,7},{9,8},{10,9},{11,1... | collective-permute-start | bytes 221192 | tf_op jit(solution)/shard_map/ppermute | solution.py:759
  9.0 7.5 %copy-start.2 = (f32[6,24,128]{2,1,0:T(8,128)}, f32[6,24,128]{2,1,0:T(8,128)S(1)}, u32[]{:S(2)}) copy-start(f32[6,24,128]{2,1,0:T(8,128)S(1)} %collective-permute-done.next_hbm) | copy-start | bytes 221188
  9.0 28.9 %all-to-all-start = ((f32[16,80,128]{2,1,0:T(8,128)}), f32[16,80,128]{2,1,0:T(8,128)S(1)}, u32[]{:S(2)}, u32[]{:S(2)}) async-start(f32[16,80,128]{2,1,0:T(8,128)} %spread.1), calls=%async_computation | async-start | bytes 1310720 | tf_op jit(solution)/shard_map/all_to_all | solution.py:761
  18.6 10.1 %collective-permute-start.1 = (f32[6,40,128]{2,1,0:T(8,128)}, f32[6,40,128]{2,1,0:T(8,128)S(1)}, u32[]{:S(2)}, u32[]{:S(2)}) collective-permute-start(f32[6,40,128]{2,1,0:T(8,128)} %get-tuple-element.20), channel_id=1, source_target_pairs={{32,64},{64,32},{96,128},{128,96},{160,192},{192,160},{224,256},{2... | collective-permute-start | bytes 368648 | tf_op jit(solution)/shard_map/ppermute | solution.py:772
  23.0 5.8 %collective-permute-start.2 = (f32[6,40,128]{2,1,0:T(8,128)}, f32[6,40,128]{2,1,0:T(8,128)S(1)}, u32[]{:S(2)}, u32[]{:S(2)}) collective-permute-start(f32[6,40,128]{2,1,0:T(8,128)} %get-tuple-element.21), channel_id=1, source_target_pairs={{0,32},{32,0},{64,96},{96,64},{128,160},{160,128},{192,224},{224,1... | collective-permute-start | bytes 368648 | tf_op jit(solution)/shard_map/ppermute | solution.py:773
  28.7 0.6 %copy-start.3 = (f32[6,40,128]{2,1,0:T(8,128)}, f32[6,40,128]{2,1,0:T(8,128)S(1)}, u32[]{:S(2)}) copy-start(f32[6,40,128]{2,1,0:T(8,128)S(1)} %collective-permute-done.1.far_hbm) | copy-start | bytes 368644
  28.7 0.7 %copy-start.4 = (f32[6,40,128]{2,1,0:T(8,128)}, f32[6,40,128]{2,1,0:T(8,128)S(1)}, u32[]{:S(2)}) copy-start(f32[6,40,128]{2,1,0:T(8,128)S(1)} %collective-permute-done.2.near_hbm) | copy-start | bytes 368644
  37.9 6.7 %copy-start.1 = (f32[16,80,128]{2,1,0:T(8,128)}, f32[16,80,128]{2,1,0:T(8,128)S(1)}, u32[]{:S(2)}) copy-start(f32[16,80,128]{2,1,0:T(8,128)S(1)} %all-to-all-done) | copy-start | bytes 1966084
  38.0 22.5 %all-to-all-start.1 = ((f32[16,80,128]{2,1,0:T(8,128)}), f32[16,80,128]{2,1,0:T(8,128)S(1)}, u32[]{:S(2)}, u32[]{:S(2)}) async-start(f32[16,80,128]{2,1,0:T(8,128)} %bitcast.3), calls=%async_computation.1 | async-start | bytes 1310720 | tf_op jit(solution)/shard_map/all_to_all | solution.py:805
  44.6 15.8 %copy-start = (f32[264]{0:T(512)S(1)}, f32[264]{0:T(512)}, u32[]{:S(2)}) copy-start(f32[264]{0:T(512)} %mass_hbm.3) | copy-start | bytes 3172
  51.4 9.0 %collective-permute-start.3 = (f32[6,24,128]{2,1,0:T(8,128)}, f32[6,24,128]{2,1,0:T(8,128)S(1)}, u32[]{:S(2)}, u32[]{:S(2)}) collective-permute-start(f32[6,24,128]{2,1,0:T(8,128)} %get-tuple-element.27), channel_id=1, source_target_pairs={{0,1},{1,2},{2,3},{3,4},{4,5},{5,6},{6,7},{7,8},{8,9},{9,10},{10,1... | collective-permute-start | bytes 221192 | tf_op jit(solution)/shard_map/ppermute | solution.py:845
